TPU v7x, 32 devices: a whole 2x2x4 slice. The times are simulated.
32 devices in a mesh: groups: 2 (over y), region: 4 (over z), lag: 2 (over x), member: 2 (over core).
Axes of the slice: x: 2, y: 2, z: 4, core: 2. Of those that a mesh axis runs over, the one named last changes fastest.
Arguments:
- snapshots: bfloat16 [4, 64, 512, 128], P(('groups', 'lag'), 'member', 'region'), parts along dimension 0, may hold values from -6 to 6
- current: float32 [128, 512, 128], P(('groups', 'lag', 'member'), 'region'), parts along dimension 0, may hold values from -6 to 6
- diffusivity: float32 [512, 128], P('region'), may hold values from 0.02 to 0.2
- landmask: int32 [512, 128], P('region'), may hold values 0 or 1
- obs_cell: int32 [65536], P(('groups', 'region')), parts along dimension 0, may hold values from 0 to 16383
- obs_value: float32 [65536], P(('groups', 'region')), parts along dimension 0, may hold values from -6 to 6
- obs_weight: float32 [65536], P(('groups', 'region')), parts along dimension 0, may hold values from 0.25 to 4
- tile_obs: int32 [1024, 512], P(('groups', 'region')), parts along dimension 0, may hold values from 0 to 24575
- tile_count: int32 [1024], P(('groups', 'region')), parts along dimension 0, may hold values from 32 to 512, as said below
Outputs:
- smoothed: bfloat16 [4, 64, 512, 128], P(('groups', 'lag'), 'member', 'region'), parts along dimension 0
- analysis: bfloat16 [128, 512, 128], P(('groups', 'lag', 'member'), 'region'), parts along dimension 0
There are 2 independent parts, one for each index of `groups`. A program takes and returns all parts, laid end to end along the dimension named above; an argument that names none is the same for every part. Nothing has to cross between parts.
Inputs may be any that keep to these rules, and one draw needn't show every extreme that they name: tile_count is skewed over tiles; some tile of every draw uses all 512 entries.
All inputs are finite; a program needn't handle non-finite values. No bound on the sum of `landmask` on one device may be relied on, other than what follows from the above.
Results may differ from a plain program's by a relative error of at most 0.012.
Values may be sent and summed in bfloat16 or wider, within the bound.
A program may use at most 128 MiB of HBM per device.

v0:
```python
import jax
import jax.numpy as jnp
from jax import lax
from jax.sharding import PartitionSpec as P

STEPS = 2


def with_halo(array, sides, width):
    for axis, dim in sides:
        size, length = (lax.axis_size(axis), array.shape[dim])
        up = [(i, (i + 1) % size) for i in range(size - 1)]
        down = [(j, i) for i, j in up]
        last = lax.slice_in_dim(array, length - width, length, axis=dim)
        leading = lax.slice_in_dim(array, 0, width, axis=dim)
        before = lax.ppermute(last, axis, up)
        after = lax.ppermute(leading, axis, down)
        array = jnp.concatenate([before, array, after], axis=dim)
    return array


def relax(padded, diffusion, sea_mask):
    centre = padded[:, 1:-1]
    upper_row = padded[:, :-2]
    lower_row = padded[:, 2:]
    right_cell = jnp.roll(centre, 1, axis=2)
    left_cell = jnp.roll(centre, -1, axis=2)
    return sea_mask * (
        centre + diffusion * (upper_row + lower_row + right_cell + left_cell - 4.0 * centre)
    )


def mixing_block(anomaly, innovation, obs_weight, window_index, live_mask):
    picked = jnp.take(anomaly, window_index, axis=1)
    obs_scale = jnp.take(obs_weight, window_index) * live_mask
    residual_obs = jnp.take(innovation, window_index)
    weighted = picked * obs_scale[None]
    members = anomaly.shape[0]
    precision_matrix = jnp.einsum(
        "mbk,nbk->bmn", weighted, picked, precision=lax.Precision.HIGHEST
    ) + (members - 1.0) * jnp.eye(members, dtype=jnp.float32)
    mean_rhs = jnp.einsum("mbk,bk->bm", weighted, residual_obs, precision=lax.Precision.HIGHEST)
    factor = jnp.linalg.cholesky(precision_matrix)
    partial_solve = jax.scipy.linalg.solve_triangular(factor, mean_rhs[:, :, None], lower=True)
    mean_weight = jax.scipy.linalg.solve_triangular(factor, partial_solve, lower=True, trans=1)[
        :, :, 0
    ]
    identity = jnp.broadcast_to(jnp.eye(members, dtype=jnp.float32), precision_matrix.shape)
    spread = jnp.sqrt(members - 1.0) * jax.scipy.linalg.solve_triangular(
        factor, identity, lower=True, trans=1
    )
    weights = spread + mean_weight[:, :, None]
    mixing = weights + (1.0 - jnp.sum(weights, axis=1, keepdims=True)) / members
    return mixing.astype(jnp.bfloat16)


def tile_mixing(anomaly, innovation, obs_weight, window_index, live_mask):
    block_count = window_index.shape[0] // 8

    def one_block(packed):
        return mixing_block(anomaly, innovation, obs_weight, packed[0], packed[1])

    mixed = lax.map(
        one_block, (window_index.reshape(block_count, 8, -1), live_mask.reshape(block_count, 8, -1))
    )
    return mixed.reshape(-1, mixed.shape[2], mixed.shape[3])


def local(
    snapshots, current, diffusivity, landmask, obs_cell, obs_value, obs_weight, tile_obs, tile_count
):
    sea_mask = landmask.astype(jnp.float32)
    field_now = current
    for substep in range(STEPS):
        padded = with_halo(field_now, (("region", 1),), 1)
        field_now = relax(padded, diffusivity, sea_mask)
    newest = field_now.astype(jnp.bfloat16)
    own_members = newest.shape[0]
    obs_count = obs_cell.shape[0]
    obs_info = jnp.stack([obs_value, obs_weight])
    window_info = with_halo(obs_info.astype(jnp.bfloat16), (("region", 1),), obs_count).astype(
        obs_info.dtype
    )
    group_size = lax.axis_size(("lag", "member"))
    group_rank = lax.axis_index(("lag", "member"))
    everyone = lax.all_gather(newest, ("lag", "member"), axis=0, tiled=True)
    sampled = jnp.take(everyone.reshape(everyone.shape[0], -1), obs_cell, axis=1)
    window_obs = with_halo(sampled, (("region", 1),), obs_count).astype(jnp.float32)
    obs_mean = jnp.mean(window_obs, axis=0)
    anomaly = window_obs - obs_mean
    innovation = window_info[0] - obs_mean
    live_mask = (
        jnp.arange(tile_obs.shape[1], dtype=jnp.int32)[None, :] < tile_count[:, None]
    ).astype(jnp.float32)
    share = tile_obs.shape[0] // group_size
    first_tile = group_rank * share
    my_index = lax.dynamic_slice_in_dim(tile_obs, first_tile, share, 0)
    my_live = lax.dynamic_slice_in_dim(live_mask, first_tile, share, 0)
    mine = tile_mixing(anomaly, innovation, window_info[1], my_index, my_live)
    mixing = lax.all_gather(mine, ("lag", "member"), axis=0, tiled=True)
    member_rank = lax.axis_index("member")
    half_members = snapshots.shape[1]
    own_columns = lax.dynamic_slice_in_dim(mixing, member_rank * half_members, half_members, 2)
    smoothed = jnp.einsum(
        "lmtc,tmn->lntc",
        lax.all_gather(snapshots, "member", axis=1, tiled=True),
        own_columns,
        preferred_element_type=jnp.float32,
    ).astype(jnp.bfloat16)
    newest_columns = lax.dynamic_slice_in_dim(mixing, group_rank * own_members, own_members, 2)
    analysis = jnp.einsum(
        "mtc,tmn->ntc", everyone, newest_columns, preferred_element_type=jnp.float32
    ).astype(jnp.bfloat16)
    return (smoothed, analysis)


def solution(mesh):
    placed = (
        P(("groups", "lag"), "member", "region", None),
        P(("groups", "lag", "member"), "region", None),
        P("region", None),
        P("region", None),
        P(("groups", "region")),
        P(("groups", "region")),
        P(("groups", "region")),
        P(("groups", "region"), None),
        P(("groups", "region")),
    )
    return jax.shard_map(
        local,
        mesh=mesh,
        in_specs=placed,
        out_specs=(
            P(("groups", "lag"), "member", "region", None),
            P(("groups", "lag", "member"), "region", None),
        ),
        check_vma=False,
    )
```

profile of v0, /device:TPU:0, one launch (start us, length us, event | category | flops | bytes accessed | tf_op | source)
XLA Modules:
  0.0 885.1 jit_solution(10046579594388050927)
XLA Ops:
  9.5 5.5 collective-permute-start.6
  31.9 4.5 collective-permute-start.2
  45.0 22.1 %all-gather.4.cloned.1.call-done = bf16[64,128,128]{2,0,1:T(8,128)(2,1)} async-done(((bf16[16,128,128]{2,0,1:T(8,128)(2,1)}), bf16[64,128,128]{2,0,1:T(8,128)(2,1)}) %all-gather.4.cloned.1.call-update) | async-done | bytes 2097168 | tf_op jit(solution)/shard_map/all_gather | solution.py:86
  67.1 4.8 copy.97
  71.9 30.9 %gather_fusion.3 = bf16[8192,64]{1,0:T(8,128)(2,1)} fusion(bf16[64,16384]{0,1:T(8,128)(2,1)} %bitcast.139, s32[8192]{0:T(1024)S(1)} %copy-done.8), kind=kCustom, calls=%fused_computation.3 | custom fusion | bytes 2129920 | tf_op jit(solution)/shard_map/jit(_take)/gather | solution.py:87
  102.8 5.8 select_bitcast_fusion.2
  116.3 20.5 %collective-permute-done.4 = bf16[64,8192]{1,0:T(8,128)(2,1)} collective-permute-done((bf16[64,8192]{1,0:T(8,128)(2,1)}, bf16[64,8192]{1,0:T(8,128)(2,1)}, u32[]{:S(2)}, u32[]{:S(2)}) %collective-permute-start.4) | collective-permute-done | bytes 1048608 | tf_op jit(solution)/shard_map/ppermute | solution.py:16
  144.6 16.7 %convert_reduce_fusion = f32[24576]{0:T(1024)S(1)} fusion(bf16[64,8192]{0,1:T(8,128)(2,1)} %copy.85, bf16[64,8192]{0,1:T(8,128)(2,1)S(1)} %select_bitcast_fusion.2, bf16[64,8192]{0,1:T(8,128)(2,1)} %copy.84), kind=kLoop, calls=%fused_computation.56 | loop fusion | flops 10985472 | bytes 3244032 | tf_op jit(solution)/shard_map/reduce_sum | solution.py:89
  161.4 46.7 %convert_subtract_fusion = f32[64,24576]{0,1:T(8,128)} fusion(f32[24576]{0:T(1024)S(1)} %get-tuple-element.84, bf16[64,8192]{0,1:T(8,128)(2,1)S(1)} %copy-done.2, bf16[64,8192]{0,1:T(8,128)(2,1)S(1)} %select_bitcast_fusion.2, bf16[64,8192]{0,1:T(8,128)(2,1)S(1)} %copy-done.1), kind=kLoop, calls=%fused_computation.55 | loop fusion | flops 11010048 | bytes 9535488 | tf_op jit(solution)/shard_map/sub | solution.py:90
  208.1 630.2 %while.10 = (s32[]{:T(128)}, bf16[4,8,64,64]{3,2,1,0:T(8,128)(2,1)S(1)}, s32[4,8,512]{2,1,0:T(8,128)S(1)}, f32[64,24576]{0,1:T(8,128)}, f32[24576]{0:T(1024)S(1)...) while((s32[]{:T(128)}, bf16[4,8,64,64]{3,2,1,0:T(8,128)(2,1)S(1)}, ...), condition=%wide.region_5.7_spmd, body=%wide.region_1.0_spmd.sunk | while | flops 232297472 | bytes 9070713 | solution.py:63
  208.1 23.0 %gather_fusion.1 = f32[4096]{0:T(1024)S(1)} fusion(f32[24576]{0:T(1024)S(1)} %get-tuple-element.162, s32[4096]{0:T(1024)S(1)} %broadcast_clamp_fusion.5), kind=kCustom, calls=%fused_computation.1.clone.clone.1 | custom fusion | bytes 49152 | tf_op jit(solution)/shard_map/while/body/eval_jaxpr/jit(_take)/gather | solution.py:36
  231.2 23.0 %gather_fusion.2 = f32[4096]{0:T(1024)S(1)} fusion(f32[24576]{0:T(1024)S(1)} %get-tuple-element.160, s32[4096]{0:T(1024)S(1)} %broadcast_clamp_fusion.5), kind=kCustom, calls=%fused_computation.clone.clone.1 | custom fusion | bytes 49152 | tf_op jit(solution)/shard_map/while/body/eval_jaxpr/jit(_take)/gather | solution.py:35
  254.3 18.8 %gather_fusion = f32[4096,64]{1,0:T(8,128)} fusion(f32[64,24576]{0,1:T(8,128)} %get-tuple-element.159, s32[4096]{0:T(1024)S(1)} %broadcast_clamp_fusion.4), kind=kCustom, calls=%fused_computation.2.clone.1 | custom fusion | bytes 2113536 | tf_op jit(solution)/shard_map/while/body/eval_jaxpr/jit(_take)/gather | solution.py:34
  276.6 46.9 %custom-call.31 = f32[8,64,64]{2,1,0:T(8,128)S(1)} custom-call(f32[8,64,64]{2,1,0:T(8,128)S(1)} %fusion.117), custom_call_target="Cholesky" | custom-call | tf_op jit(solution)/shard_map/while/body/eval_jaxpr/jit(cholesky)/cholesky | solution.py:43
  323.8 39.3 %custom-call.32 = f32[8,1,64,64]{2,3,1,0:T(8,128)S(1)} custom-call(f32[8,1,64,64]{3,2,1,0:T(8,128)S(1)} %select_bitcast_fusion.6), custom_call_target="InvertDiagBlocksLowerTriangular" | custom-call | tf_op jit(solution)/shard_map/while/body/eval_jaxpr/jit(_solve_triangular)/vmap()/triangular_solve | solution.py:49
  365.6 23.0 %gather_fusion.1 = f32[4096]{0:T(1024)S(1)} fusion(f32[24576]{0:T(1024)S(1)} %get-tuple-element.162, s32[4096]{0:T(1024)S(1)} %broadcast_clamp_fusion.5), kind=kCustom, calls=%fused_computation.1.clone.clone.1 | custom fusion | bytes 49152 | tf_op jit(solution)/shard_map/while/body/eval_jaxpr/jit(_take)/gather | solution.py:36
  388.7 23.0 %gather_fusion.2 = f32[4096]{0:T(1024)S(1)} fusion(f32[24576]{0:T(1024)S(1)} %get-tuple-element.160, s32[4096]{0:T(1024)S(1)} %broadcast_clamp_fusion.5), kind=kCustom, calls=%fused_computation.clone.clone.1 | custom fusion | bytes 49152 | tf_op jit(solution)/shard_map/while/body/eval_jaxpr/jit(_take)/gather | solution.py:35
  411.8 18.8 %gather_fusion = f32[4096,64]{1,0:T(8,128)} fusion(f32[64,24576]{0,1:T(8,128)} %get-tuple-element.159, s32[4096]{0:T(1024)S(1)} %broadcast_clamp_fusion.4), kind=kCustom, calls=%fused_computation.2.clone.1 | custom fusion | bytes 2113536 | tf_op jit(solution)/shard_map/while/body/eval_jaxpr/jit(_take)/gather | solution.py:34
  434.2 46.9 %custom-call.31 = f32[8,64,64]{2,1,0:T(8,128)S(1)} custom-call(f32[8,64,64]{2,1,0:T(8,128)S(1)} %fusion.117), custom_call_target="Cholesky" | custom-call | tf_op jit(solution)/shard_map/while/body/eval_jaxpr/jit(cholesky)/cholesky | solution.py:43
  481.4 39.3 %custom-call.32 = f32[8,1,64,64]{2,3,1,0:T(8,128)S(1)} custom-call(f32[8,1,64,64]{3,2,1,0:T(8,128)S(1)} %select_bitcast_fusion.6), custom_call_target="InvertDiagBlocksLowerTriangular" | custom-call | tf_op jit(solution)/shard_map/while/body/eval_jaxpr/jit(_solve_triangular)/vmap()/triangular_solve | solution.py:49
  523.2 23.0 %gather_fusion.1 = f32[4096]{0:T(1024)S(1)} fusion(f32[24576]{0:T(1024)S(1)} %get-tuple-element.162, s32[4096]{0:T(1024)S(1)} %broadcast_clamp_fusion.5), kind=kCustom, calls=%fused_computation.1.clone.clone.1 | custom fusion | bytes 49152 | tf_op jit(solution)/shard_map/while/body/eval_jaxpr/jit(_take)/gather | solution.py:36
  546.3 23.0 %gather_fusion.2 = f32[4096]{0:T(1024)S(1)} fusion(f32[24576]{0:T(1024)S(1)} %get-tuple-element.160, s32[4096]{0:T(1024)S(1)} %broadcast_clamp_fusion.5), kind=kCustom, calls=%fused_computation.clone.clone.1 | custom fusion | bytes 49152 | tf_op jit(solution)/shard_map/while/body/eval_jaxpr/jit(_take)/gather | solution.py:35
  569.4 18.8 %gather_fusion = f32[4096,64]{1,0:T(8,128)} fusion(f32[64,24576]{0,1:T(8,128)} %get-tuple-element.159, s32[4096]{0:T(1024)S(1)} %broadcast_clamp_fusion.4), kind=kCustom, calls=%fused_computation.2.clone.1 | custom fusion | bytes 2113536 | tf_op jit(solution)/shard_map/while/body/eval_jaxpr/jit(_take)/gather | solution.py:34
  591.7 46.9 %custom-call.31 = f32[8,64,64]{2,1,0:T(8,128)S(1)} custom-call(f32[8,64,64]{2,1,0:T(8,128)S(1)} %fusion.117), custom_call_target="Cholesky" | custom-call | tf_op jit(solution)/shard_map/while/body/eval_jaxpr/jit(cholesky)/cholesky | solution.py:43
  638.9 39.3 %custom-call.32 = f32[8,1,64,64]{2,3,1,0:T(8,128)S(1)} custom-call(f32[8,1,64,64]{3,2,1,0:T(8,128)S(1)} %select_bitcast_fusion.6), custom_call_target="InvertDiagBlocksLowerTriangular" | custom-call | tf_op jit(solution)/shard_map/while/body/eval_jaxpr/jit(_solve_triangular)/vmap()/triangular_solve | solution.py:49
  680.7 23.0 %gather_fusion.1 = f32[4096]{0:T(1024)S(1)} fusion(f32[24576]{0:T(1024)S(1)} %get-tuple-element.162, s32[4096]{0:T(1024)S(1)} %broadcast_clamp_fusion.5), kind=kCustom, calls=%fused_computation.1.clone.clone.1 | custom fusion | bytes 49152 | tf_op jit(solution)/shard_map/while/body/eval_jaxpr/jit(_take)/gather | solution.py:36
  703.8 23.0 %gather_fusion.2 = f32[4096]{0:T(1024)S(1)} fusion(f32[24576]{0:T(1024)S(1)} %get-tuple-element.160, s32[4096]{0:T(1024)S(1)} %broadcast_clamp_fusion.5), kind=kCustom, calls=%fused_computation.clone.clone.1 | custom fusion | bytes 49152 | tf_op jit(solution)/shard_map/while/body/eval_jaxpr/jit(_take)/gather | solution.py:35
  726.9 18.8 %gather_fusion = f32[4096,64]{1,0:T(8,128)} fusion(f32[64,24576]{0,1:T(8,128)} %get-tuple-element.159, s32[4096]{0:T(1024)S(1)} %broadcast_clamp_fusion.4), kind=kCustom, calls=%fused_computation.2.clone.1 | custom fusion | bytes 2113536 | tf_op jit(solution)/shard_map/while/body/eval_jaxpr/jit(_take)/gather | solution.py:34
  749.3 46.9 %custom-call.31 = f32[8,64,64]{2,1,0:T(8,128)S(1)} custom-call(f32[8,64,64]{2,1,0:T(8,128)S(1)} %fusion.117), custom_call_target="Cholesky" | custom-call | tf_op jit(solution)/shard_map/while/body/eval_jaxpr/jit(cholesky)/cholesky | solution.py:43
  796.5 39.3 %custom-call.32 = f32[8,1,64,64]{2,3,1,0:T(8,128)S(1)} custom-call(f32[8,1,64,64]{3,2,1,0:T(8,128)S(1)} %select_bitcast_fusion.6), custom_call_target="InvertDiagBlocksLowerTriangular" | custom-call | tf_op jit(solution)/shard_map/while/body/eval_jaxpr/jit(_solve_triangular)/vmap()/triangular_solve | solution.py:49
  842.0 18.4 %all-gather.6.cloned.1.call-done = bf16[128,64,64]{2,1,0:T(8,128)(2,1)} async-done(((bf16[32,64,64]{2,1,0:T(8,128)(2,1)}), bf16[128,64,64]{2,1,0:T(8,128)(2,1)}) %all-gather.6.cloned.1.call-update) | async-done | bytes 1048592 | tf_op jit(solution)/shard_map/all_gather | solution.py:100
  864.8 8.4 all-gather.8.cloned.1.call-done
  (181 shorter events, 81.6 us)
Async XLA Ops:
  7.2 36.9 %copy-start = (s32[128,512]{1,0:T(8,128)S(1)}, s32[128,512]{1,0:T(8,128)}, u32[]{:S(2)}) copy-start(s32[128,512]{1,0:T(8,128)} %param.20) | copy-start | bytes 786436
  7.2 59.9 %all-gather.4.cloned.1.call-start = ((), (), s32[]{:S(2)}) async-start(), calls=%async_computation | async-start | bytes 2621440 | tf_op jit(solution)/shard_map/all_gather | solution.py:86
  8.8 6.2 copy-start.5
  9.5 34.5 %collective-permute-start.6 = (bf16[2,8192]{1,0:T(2,128)(2,1)}, bf16[2,8192]{1,0:T(2,128)(2,1)}, u32[]{:S(2)}, u32[]{:S(2)}) collective-permute-start(bf16[2,8192]{1,0:T(2,128)(2,1)} %pad_maximum_fusion.5), channel_id=1, source_target_pairs={{0,4},{4,8},{8,12},{1,5},{5,9},{9,13},{2,6},{6,10},{10,14},{3,7},{... | collective-permute-start | bytes 98312 | tf_op jit(solution)/shard_map/ppermute | solution.py:16
  15.1 29.0 %collective-permute-start.7 = (bf16[2,8192]{1,0:T(2,128)(2,1)}, bf16[2,8192]{1,0:T(2,128)(2,1)}, u32[]{:S(2)}, u32[]{:S(2)}) collective-permute-start(bf16[2,8192]{1,0:T(2,128)(2,1)} %pad_maximum_fusion.5), channel_id=1, source_target_pairs={{4,0},{8,4},{12,8},{5,1},{9,5},{13,9},{6,2},{10,6},{14,10},{7,3},{... | collective-permute-start | bytes 98312 | tf_op jit(solution)/shard_map/ppermute | solution.py:17
  18.8 10.6 %collective-permute-start = (f32[16,1,128]{2,0,1:T(8,128)}, f32[16,1,128]{2,0,1:T(8,128)S(1)}, u32[]{:S(2)}, u32[]{:S(2)}) collective-permute-start(f32[16,1,128]{2,0,1:T(8,128)} %get-tuple-element.79), channel_id=1, source_target_pairs={{0,4},{4,8},{8,12},{1,5},{5,9},{9,13},{2,6},{6,10},{10,14},{3,7},{... | collective-permute-start | bytes 24584 | tf_op jit(solution)/shard_map/ppermute | solution.py:16
  23.3 6.1 collective-permute-start.1
  25.0 1.7 copy-start.9
  31.9 6.3 collective-permute-start.2
  36.5 5.7 copy-start.7
  36.5 5.7 collective-permute-start.3
  42.2 1.8 copy-start.10
  42.2 1.9 copy-start.6
  43.9 816.6 %all-gather.6.cloned.1.call-start = ((), (), s32[]{:S(2)}) async-start(), calls=%async_computation.1 | async-start | bytes 2621440 | tf_op jit(solution)/shard_map/all_gather | solution.py:100
  45.0 26.9 %copy-start.8 = (s32[8192]{0:T(1024)S(1)}, s32[8192]{0:T(1024)}, u32[]{:S(2)}) copy-start(s32[8192]{0:T(1024)} %fusion.71) | copy-start | bytes 98308
  110.3 26.5 %collective-permute-start.4 = (bf16[64,8192]{1,0:T(8,128)(2,1)}, bf16[64,8192]{1,0:T(8,128)(2,1)}, u32[]{:S(2)}, u32[]{:S(2)}) collective-permute-start(bf16[64,8192]{1,0:T(8,128)(2,1)} %copy.82), channel_id=1, source_target_pairs={{0,4},{4,8},{8,12},{1,5},{5,9},{9,13},{2,6},{6,10},{10,14},{3,7},{... | collective-permute-start | bytes 3145736 | tf_op jit(solution)/shard_map/ppermute | solution.py:16
  114.6 27.2 %collective-permute-start.5 = (bf16[64,8192]{1,0:T(8,128)(2,1)}, bf16[64,8192]{1,0:T(8,128)(2,1)}, u32[]{:S(2)}, u32[]{:S(2)}) collective-permute-start(bf16[64,8192]{1,0:T(8,128)(2,1)} %copy.82), channel_id=1, source_target_pairs={{4,0},{8,4},{12,8},{5,1},{9,5},{13,9},{6,2},{10,6},{14,10},{7,3},{... | collective-permute-start | bytes 3145736 | tf_op jit(solution)/shard_map/ppermute | solution.py:17
  144.6 16.8 %copy-start.1 = (bf16[64,8192]{0,1:T(8,128)(2,1)S(1)}, bf16[64,8192]{0,1:T(8,128)(2,1)}, u32[]{:S(2)}) copy-start(bf16[64,8192]{0,1:T(8,128)(2,1)} %copy.84) | copy-start | bytes 3145732
  144.6 16.8 %copy-start.2 = (bf16[64,8192]{0,1:T(8,128)(2,1)S(1)}, bf16[64,8192]{0,1:T(8,128)(2,1)}, u32[]{:S(2)}) copy-start(bf16[64,8192]{0,1:T(8,128)(2,1)} %copy.85) | copy-start | bytes 3145732
  838.2 0.8 copy-start.4
  838.3 22.2 %copy-start.3 = (bf16[64,128,128]{2,0,1:T(8,128)(2,1)S(1)}, bf16[64,128,128]{2,0,1:T(8,128)(2,1)}, u32[]{:S(2)}) copy-start(bf16[64,128,128]{2,0,1:T(8,128)(2,1)} %all-gather.4.cloned.1.call-done) | copy-start | bytes 6291460
  839.1 34.1 %all-gather.8.cloned.1.call-start = ((), (), s32[]{:S(2)}) async-start(), calls=%async_computation.2 | async-start | bytes 3145728 | tf_op jit(solution)/shard_map/all_gather | solution.py:106
Sparse Core Ops, SparseCore 0:
  44.0 23.0 all-gather.3
  839.2 21.2 all-gather.5
  862.6 10.5 all-gather.7
where the time goes:
time: 886 us; the launch traced here: 885 us
  other arithmetic  424 us (48%)
  local copies, waits for them, and re-layouts  324 us (37%)
  waiting for transfers between devices  75.8 us (9%)
  starting transfers between devices  24.6 us (3%)
  matrix products  21.5 us (2%)
  between operations  14 us (2%)
    another operation x16, other arithmetic, mixing_block(): factor = jnp.linalg.cholesky(precision_matrix)  188 us
    another operation x12, other arithmetic, mixing_block(): jax.scipy.linalg.solve_triangular(factor, identity, lower=True, trans=1)  158 us
    gather x8, local copies, waits for them, and re-layouts, mixing_block(): residual_obs = jnp.take(innovation, window_index)  92.1 us
    gather x8, local copies, waits for them, and re-layouts, mixing_block(): obs_scale = jnp.take(obs_weight, window_index) * live_mask  92.1 us
    gather x8, local copies, waits for them, and re-layouts, mixing_block(): picked = jnp.take(anomaly, window_index, axis=1)  83.7 us
    sub x1, other arithmetic, local(): anomaly = window_obs - obs_mean  46.7 us
    gather x1, local copies, waits for them, and re-layouts, local(): jnp.take(everyone.reshape(everyone.shape[0], -1), obs_cell, axis=1)  30.9 us
    all_gather x1, waiting for transfers between devices, local(): everyone = lax.all_gather(newest, ('lag', 'member'), axis=0, tiled=True)  22.1 us
  transfers between devices with their start and end apart: 11, of which 6 were waited for; matrix products, arithmetic and copies ran while one was open for 3% of the time, Pallas kernels for 0%

commit v1 on v0

v1 whole, which is shorter than its diff:
```python
import functools

import jax
import jax.numpy as jnp
from jax import lax
from jax.experimental import pallas as pl
from jax.experimental.pallas import tpu as pltpu
from jax.sharding import PartitionSpec as P

STEPS = 2
LANES = 128
VMEM_BYTES = 56 * 1024 * 1024


def with_halo(array, sides, width):
    for axis, dim in sides:
        size, length = (lax.axis_size(axis), array.shape[dim])
        up = [(i, (i + 1) % size) for i in range(size - 1)]
        down = [(j, i) for i, j in up]
        last = lax.slice_in_dim(array, length - width, length, axis=dim)
        leading = lax.slice_in_dim(array, 0, width, axis=dim)
        before = lax.ppermute(last, axis, up)
        after = lax.ppermute(leading, axis, down)
        array = jnp.concatenate([before, array, after], axis=dim)
    return array


def relax(padded, diffusion, sea_mask):
    centre = padded[:, 1:-1]
    upper_row = padded[:, :-2]
    lower_row = padded[:, 2:]
    right_cell = jnp.roll(centre, 1, axis=2)
    left_cell = jnp.roll(centre, -1, axis=2)
    return sea_mask * (
        centre + diffusion * (upper_row + lower_row + right_cell + left_cell - 4.0 * centre)
    )


NT = (((1,), (1,)), ((), ()))
TN = (((0,), (0,)), ((), ()))


def identity():
    row = lax.broadcasted_iota(jnp.int32, (LANES, LANES), 0)
    col = lax.broadcasted_iota(jnp.int32, (LANES, LANES), 1)
    return (row == col).astype(jnp.bfloat16)


def vmem_call(kernel, out_shape, scratch_shapes, in_spaces, flops):
    return pl.pallas_call(
        kernel,
        out_shape=out_shape,
        in_specs=[pl.BlockSpec(memory_space=space) for space in in_spaces],
        out_specs=jax.tree.map(lambda _: pl.BlockSpec(memory_space=pltpu.VMEM), out_shape),
        scratch_shapes=scratch_shapes,
        compiler_params=pltpu.CompilerParams(vmem_limit_bytes=VMEM_BYTES),
        cost_estimate=pl.CostEstimate(flops=flops, bytes_accessed=1 << 22, transcendentals=0),
    )


def sample_kernel(cell_ref, field_ref, out_ref, table, picked):
    owners, rows, own, cols = field_ref.shape
    members = owners * own
    eye = identity()

    def build(r, carry):
        part = field_ref[:, r].reshape(members, cols)
        table[pl.ds(pl.multiple_of(r * cols, cols), cols), :members] = lax.dot_general(
            eye, part, NT, preferred_element_type=jnp.float32
        )
        return carry

    lax.fori_loop(0, rows, build, 0, unroll=4)
    picked[:, members:] = jnp.zeros((LANES, LANES - members), jnp.float32)

    def block(b, carry):
        base = pl.multiple_of(b * LANES, LANES)

        def rows16(g, inner):
            for q in range(16):
                k = g * 16 + q
                picked[pl.ds(k, 1), :members] = table[pl.ds(cell_ref[base + k], 1), :members]
            return inner

        lax.fori_loop(0, LANES // 16, rows16, 0, unroll=True)
        flipped = picked[...].T
        out_ref[:, pl.ds(base, LANES)] = flipped[:members].astype(jnp.bfloat16)
        return carry

    lax.fori_loop(0, cell_ref.shape[0] // LANES, block, 0)


def mixing_kernel(
    count_ref, index_ref, before_ref, own_ref, after_ref, info_ref, out_ref,
    table, picked, gram, chol, inv, wide,
):
    share = count_ref.shape[0]
    entries = index_ref.shape[0] // share
    members, obs = own_ref.shape
    blocks = obs // LANES
    eye = identity()

    for part, ref in enumerate((before_ref, own_ref, after_ref)):

        def build(b, carry, part=part, ref=ref):
            sample = ref[:, pl.ds(pl.multiple_of(b * LANES, LANES), LANES)].astype(jnp.float32)
            mean = jnp.sum(sample, axis=0, keepdims=True) * (1.0 / members)
            value = info_ref[0, pl.ds(part * blocks + b, 1), :]
            weight = info_ref[1, pl.ds(part * blocks + b, 1), :]
            row = lax.broadcasted_iota(jnp.int32, (LANES - members, LANES), 0)
            extra = jnp.where(row == 0, value - mean, jnp.where(row == 1, weight, 0.0))
            rows = jnp.concatenate([sample - mean, extra], axis=0).astype(jnp.bfloat16)
            table[pl.ds(pl.multiple_of((part * blocks + b) * LANES, LANES), LANES), :] = (
                lax.dot_general(eye, rows, NT, preferred_element_type=jnp.float32)
            )
            return carry

        lax.fori_loop(0, blocks, build, 0, unroll=4)

    def tile(t, carry):
        count = count_ref[t]
        first = t * entries

        def rows16(g, inner):
            for q in range(16):
                k = g * 16 + q
                picked[pl.ds(k, 1), :] = table[pl.ds(index_ref[first + k], 1), :]
            return inner

        lax.fori_loop(0, (count + 15) // 16, rows16, 0)

        def chunk(c, total):
            base = pl.multiple_of(c * LANES, LANES)
            rows = picked[pl.ds(base, LANES), :]
            live = lax.broadcasted_iota(jnp.int32, (LANES, LANES), 0) + base < count
            rows = jnp.where(live, rows, 0.0)
            scaled = (rows * rows[:, members + 1 : members + 2]).astype(jnp.bfloat16)
            return total + lax.dot_general(
                rows.astype(jnp.bfloat16), scaled, TN, preferred_element_type=jnp.float32
            )

        gram[t] = lax.fori_loop(
            0, (count + LANES - 1) // LANES, chunk, jnp.zeros((LANES, LANES), jnp.float32)
        )
        return carry

    lax.fori_loop(0, share, tile, 0)

    copies = LANES // share

    def in_lanes(m):
        return jnp.concatenate([gram[:, m, :]] * copies, axis=0).T[:members]

    row_id = lax.broadcasted_iota(jnp.int32, (members, LANES), 0)
    for m in range(members):
        chol[m] = in_lanes(m) + jnp.where(row_id == m, members - 1.0, 0.0)
    rhs = in_lanes(members)

    width = 4
    for p in range(members // width):
        low = p * width // 8 * 8
        columns = [chol[p * width + q, low:, :] for q in range(width)]

        def eliminate(j, cols, p=p, low=low):
            left = chol[j, low:, :]
            return tuple(
                cols[q] - left * left[p * width + q - low : p * width + q - low + 1]
                for q in range(width)
            )

        columns = list(lax.fori_loop(0, p * width, eliminate, tuple(columns)))
        for q in range(width):
            at = p * width + q - low
            columns[q] = columns[q] * lax.rsqrt(columns[q][at : at + 1])
            for later in range(q + 1, width):
                spot = p * width + later - low
                columns[later] = columns[later] - columns[q] * columns[q][spot : spot + 1]
            chol[p * width + q, low:, :] = columns[q]

    for p in range(members // width):
        high = (p * width // 8 + 1) * 8
        ids = row_id[:high]
        rows = [jnp.where(ids == p * width + q, 1.0, 0.0) for q in range(width)]

        def substitute(j, rows, p=p, high=high):
            solved = inv[j, :high, :]
            group = chol[j, pl.ds(p * width // 8 * 8, 8), :]
            at = p * width % 8
            return tuple(
                rows[q] - solved * group[at + q : at + q + 1] for q in range(width)
            )

        rows = list(lax.fori_loop(0, p * width, substitute, tuple(rows)))
        for q in range(width):
            n = p * width + q
            rows[q] = rows[q] / chol[n, n : n + 1, :]
            for later in range(q + 1, width):
                spot = p * width + later
                rows[later] = rows[later] - rows[q] * chol[n, spot : spot + 1, :]
            inv[n, :high, :] = rows[q]
            if high < members:
                inv[n, high:, :] = jnp.zeros((members - high, LANES), jnp.float32)

    def apply(n, mean_weight):
        solved = inv[n]
        return mean_weight + solved * jnp.sum(solved * rhs, axis=0, keepdims=True)

    mean_weight = lax.fori_loop(0, members, apply, jnp.zeros((members, LANES), jnp.float32))
    root = float(members - 1) ** 0.5
    for n in range(members):
        weights = root * inv[n] + mean_weight
        mixed = weights + (1.0 - jnp.sum(weights, axis=0, keepdims=True)) * (1.0 / members)
        wide[:, n, :] = mixed.T[:share]
    out_ref[...] = wide[...].astype(jnp.bfloat16)


def update_kernel(snap_ref, snap_mix_ref, field_ref, field_mix_ref, smooth_ref, analysis_ref):
    owners, tiles, own, cols = field_ref.shape

    def tile(t, carry):
        smooth_ref[t] = jnp.dot(
            snap_mix_ref[t],
            snap_ref[:, t].reshape(owners * own, cols),
            preferred_element_type=jnp.float32,
        ).astype(jnp.bfloat16)
        analysis_ref[t] = jnp.dot(
            field_mix_ref[t],
            field_ref[:, t].reshape(owners * own, cols),
            preferred_element_type=jnp.float32,
        ).astype(jnp.bfloat16)
        return carry

    lax.fori_loop(0, tiles, tile, 0, unroll=4)


def halo_parts(array, axis, dim, width):
    size, length = lax.axis_size(axis), array.shape[dim]
    up = [(i, (i + 1) % size) for i in range(size - 1)]
    down = [(j, i) for i, j in up]
    before = lax.ppermute(lax.slice_in_dim(array, length - width, length, axis=dim), axis, up)
    after = lax.ppermute(lax.slice_in_dim(array, 0, width, axis=dim), axis, down)
    return before, after


def local(
    snapshots, current, diffusivity, landmask, obs_cell, obs_value, obs_weight, tile_obs, tile_count
):
    sea_mask = landmask.astype(jnp.float32)
    field_now = current
    for substep in range(STEPS):
        padded = with_halo(field_now, (("region", 1),), 1)
        field_now = relax(padded, diffusivity, sea_mask)
    newest = field_now.astype(jnp.bfloat16)
    own_members = newest.shape[0]
    obs_count = obs_cell.shape[0]
    obs_info = jnp.stack([obs_value, obs_weight])
    window_info = with_halo(obs_info.astype(jnp.bfloat16), (("region", 1),), obs_count).astype(
        obs_info.dtype
    )
    group_size = lax.axis_size(("lag", "member"))
    group_rank = lax.axis_index(("lag", "member"))
    by_row = newest.transpose(1, 0, 2)
    everyone = lax.all_gather(by_row, ("lag", "member"), axis=0)
    members = group_size * own_members
    vmem, smem = pltpu.VMEM, pltpu.SMEM
    rows, cols = newest.shape[1:]
    sampled = vmem_call(
        sample_kernel,
        jax.ShapeDtypeStruct((members, obs_count), jnp.bfloat16),
        [pltpu.VMEM((rows * cols, LANES), jnp.float32), pltpu.VMEM((LANES, LANES), jnp.float32)],
        (smem, vmem),
        10**8,
    )(obs_cell, everyone)
    before, after = halo_parts(sampled, "region", 1, obs_count)
    share = tile_obs.shape[0] // group_size
    first_tile = group_rank * share
    my_index = lax.dynamic_slice_in_dim(tile_obs, first_tile, share, 0).reshape(-1)
    my_count = lax.dynamic_slice_in_dim(tile_count, first_tile, share, 0)
    mine = vmem_call(
        mixing_kernel,
        jax.ShapeDtypeStruct((share, members, members), jnp.bfloat16),
        [
            pltpu.VMEM((3 * obs_count, LANES), jnp.float32),
            pltpu.VMEM((tile_obs.shape[1], LANES), jnp.float32),
            pltpu.VMEM((share, LANES, LANES), jnp.float32),
            pltpu.VMEM((members, members, LANES), jnp.float32),
            pltpu.VMEM((members, members, LANES), jnp.float32),
            pltpu.VMEM((share, members, members), jnp.float32),
        ],
        (smem, smem, vmem, vmem, vmem, vmem),
        10**9,
    )(my_count, my_index, before, sampled, after, window_info.reshape(2, -1, LANES))
    mixing = lax.all_gather(mine, ("lag", "member"), axis=0, tiled=True)
    member_rank = lax.axis_index("member")
    half_members = snapshots.shape[1]
    snap_mix = lax.dynamic_slice_in_dim(mixing, member_rank * half_members, half_members, 1)
    field_mix = lax.dynamic_slice_in_dim(mixing, group_rank * own_members, own_members, 1)
    snaps = lax.all_gather(snapshots[0].transpose(1, 0, 2), "member", axis=0)
    smoothed, analysis = vmem_call(
        update_kernel,
        (
            jax.ShapeDtypeStruct((rows, half_members, cols), jnp.bfloat16),
            jax.ShapeDtypeStruct((rows, own_members, cols), jnp.bfloat16),
        ),
        [],
        (vmem,) * 4,
        10**8,
    )(snaps, snap_mix, everyone, field_mix)
    return (smoothed.transpose(1, 0, 2)[None], analysis.transpose(1, 0, 2))


def solution(mesh):
    placed = (
        P(("groups", "lag"), "member", "region", None),
        P(("groups", "lag", "member"), "region", None),
        P("region", None),
        P("region", None),
        P(("groups", "region")),
        P(("groups", "region")),
        P(("groups", "region")),
        P(("groups", "region"), None),
        P(("groups", "region")),
    )
    return jax.shard_map(
        local,
        mesh=mesh,
        in_specs=placed,
        out_specs=(
            P(("groups", "lag"), "member", "region", None),
            P(("groups", "lag", "member"), "region", None),
        ),
        check_vma=False,
    )
```

time: 886 us -> 211 us (0.24)
  other arithmetic: 424 us -> 3.19 us
  local copies, waits for them, and re-layouts: 324 us -> 23.4 us
  Pallas kernels: 0 us -> 81.9 us
  matrix products: 21.5 us -> 0 us
  waiting for transfers between devices: 75.8 us -> 64.9 us
    another operation x30 -> x2, other arithmetic: 348 us -> 0.01 us  [the longest x16 188 us: mixing_block(): factor = jnp.linalg.cholesky(precision_matrix)]
    gather x25 -> x0, local copies, waits for them, and re-layouts: 299 us -> none  [the longest x8 92.1 us: mixing_block(): residual_obs = jnp.take(innovation, window_index)]
    pallas_call x0 -> x3, Pallas kernels: none -> 81.9 us  [the longest x1 53.3 us: local(): vmem_call(mixing_kernel, jax.ShapeDtypeStruct((share, members, members),...]
    sub x2 -> x0, other arithmetic: 46.7 us -> none  [the longest x1 46.7 us: local(): anomaly = window_obs - obs_mean]
    ppermute x4 -> x3, waiting for transfers between devices: 20.5 us -> 0.01 us  [with_halo(): before = lax.ppermute(last, axis, up)]
    ppermute x4 -> x3, waiting for transfers between devices: 6.26 us -> 24 us  [with_halo(): after = lax.ppermute(leading, axis, down)]
    reduce_sum x1 -> x0, other arithmetic: 16.7 us -> none  [local(): obs_mean = jnp.mean(window_obs, axis=0)]
    dot_general x10 -> x0, matrix products: 16.4 us -> none  [the longest x4 4.7 us: mixing_block(): jnp.einsum('mbk,nbk->bmn', weighted, picked, precision=lax.Precision.HIGH...]
  transfers between devices with their start and end apart: 11 -> 11, of which waited for: 6 -> 5; matrix products, arithmetic and copies ran while one was open for 3% -> 6% of each run, Pallas kernels for 0% -> 35%
where the time goes in v1:
time: 211 us; the launch traced here: 210 us
  Pallas kernels  81.9 us (39%)
  waiting for transfers between devices  64.9 us (31%)
  local copies, waits for them, and re-layouts  23.4 us (11%)
  starting transfers between devices  22.4 us (11%)
  between operations  14 us (7%)
  other arithmetic  3.19 us (2%)
    pallas_call x1, Pallas kernels, local(): vmem_call(mixing_kernel, jax.ShapeDtypeStruct((share, members, members),...  53.3 us
    ppermute x3, waiting for transfers between devices, with_halo(): after = lax.ppermute(leading, axis, down)  24 us
    all_gather x1, waiting for transfers between devices, local(): everyone = lax.all_gather(by_row, ('lag', 'member'), axis=0)  21.7 us
    pallas_call x1, Pallas kernels, local(): vmem_call(sample_kernel, jax.ShapeDtypeStruct((members, obs_count), jnp.b...  19.8 us
    all_gather x1, waiting for transfers between devices, local(): mixing = lax.all_gather(mine, ('lag', 'member'), axis=0, tiled=True)  18.5 us
    ppermute x3, starting transfers between devices, with_halo(): before = lax.ppermute(last, axis, up)  13.6 us
    pallas_call x1, Pallas kernels, local(): vmem_call(update_kernel, (jax.ShapeDtypeStruct((rows, half_members, cols)...  8.84 us
    unnamed x26, local copies, waits for them, and re-layouts  6.13 us
  transfers between devices with their start and end apart: 11, of which 5 were waited for; matrix products, arithmetic and copies ran while one was open for 6% of the time, Pallas kernels for 35%

profile of v1, /device:TPU:0, one launch (start us, length us, event | category | flops | bytes accessed | tf_op | source)
XLA Modules:
  0.0 210.0 jit_solution(10560490695674116193)
XLA Ops:
  7.2 0.9 fusion.21
  8.1 4.9 %collective-permute-start = (f32[16,1,128]{2,1,0:T(1,128)S(1)}, f32[16,1,128]{2,1,0:T(1,128)S(1)}, u32[]{:S(2)}, u32[]{:S(2)}) collective-permute-start(f32[16,1,128]{2,1,0:T(1,128)S(1)} %get-tuple-element.20), channel_id=1, source_target_pairs={{0,4},{4,8},{8,12},{1,5},{5,9},{9,13},{2,6},{6,10},{10,14},{3,7},{... | collective-permute-start | bytes 24584 | tf_op jit(solution)/shard_map/ppermute | solution.py:22
  13.1 1.4 collective-permute-start.1
  14.5 1.9 fusion.19
  16.8 0.5 copy-done.8
  17.3 1.5 collective-permute-done.1
  18.8 0.8 fusion.14
  19.9 3.5 %collective-permute-start.2 = (f32[16,1,128]{2,1,0:T(1,128)S(1)}, f32[16,1,128]{2,1,0:T(1,128)S(1)}, u32[]{:S(2)}, u32[]{:S(2)}) collective-permute-start(f32[16,1,128]{2,1,0:T(1,128)S(1)} %get-tuple-element.10), channel_id=1, source_target_pairs={{0,4},{4,8},{8,12},{1,5},{5,9},{9,13},{2,6},{6,10},{10,14},{3,7},{... | collective-permute-start | bytes 24584 | tf_op jit(solution)/shard_map/ppermute | solution.py:22
  23.4 1.3 collective-permute-start.3
  25.1 3.9 %collective-permute-done.3 = f32[16,1,128]{2,1,0:T(1,128)S(1)} collective-permute-done((f32[16,1,128]{2,1,0:T(1,128)S(1)}, f32[16,1,128]{2,1,0:T(1,128)S(1)}, u32[]{:S(2)}, u32[]{:S(2)}) %collective-permute-start.3) | collective-permute-done | bytes 8224 | tf_op jit(solution)/shard_map/ppermute | solution.py:23
  29.0 1.6 fusion.15
  30.7 0.7 all-gather.8.cloned.1.call-update
  31.5 21.7 %all-gather.10.cloned.1.call-done = bf16[512,16,128]{2,0,1:T(8,128)(2,1)} async-done(((bf16[128,16,128]{2,0,1:T(8,128)(2,1)}), bf16[512,16,128]{2,0,1:T(8,128)(2,1)}) %all-gather.10.cloned.1.call-update) | async-done | bytes 2097168 | tf_op jit(solution)/shard_map/all_gather | solution.py:263
  53.2 4.3 %copy.16 = bf16[512,16,128]{2,1,0:T(8,128)(2,1)} copy(bf16[512,16,128]{2,0,1:T(8,128)(2,1)} %all-gather.10.cloned.1.call-done) | data formatting | bytes 4194304 | tf_op jit(solution)/shard_map/all_gather | solution.py:263
  57.5 19.8 %shard_map.104.own_ref = bf16[64,8192]{1,0:T(8,128)(2,1)} custom-call(s32[8192]{0:T(1024)} %cell_ref.1, bf16[4,128,16,128]{3,2,1,0:T(8,128)(2,1)} %bitcast.26), custom_call_target="tpu_custom_call" | custom-call | flops 100000000 | bytes 4194304 | tf_op jit(solution)/shard_map/pallas_call | solution.py:267
  77.3 3.4 %collective-permute-start.4 = (bf16[64,8192]{1,0:T(8,128)(2,1)}, bf16[64,8192]{1,0:T(8,128)(2,1)S(1)}, u32[]{:S(2)}, u32[]{:S(2)}) collective-permute-start(bf16[64,8192]{1,0:T(8,128)(2,1)} %shard_map.104.own_ref), channel_id=1, source_target_pairs={{0,4},{4,8},{8,12},{1,5},{5,9},{9,13},{2,6},{6,10},{10,14},{3,7},{... | collective-permute-start | bytes 3145736 | tf_op jit(solution)/shard_map/ppermute | solution.py:240
  80.8 1.3 collective-permute-start.5
  82.2 1.3 collective-permute-start.7
  83.5 5.2 %collective-permute-start.6 = (bf16[2,8192]{1,0:T(2,128)(2,1)S(1)}, bf16[2,8192]{1,0:T(2,128)(2,1)S(1)}, u32[]{:S(2)}, u32[]{:S(2)}) collective-permute-start(bf16[2,8192]{1,0:T(2,128)(2,1)S(1)} %pad_maximum_fusion.4), channel_id=1, source_target_pairs={{0,4},{4,8},{8,12},{1,5},{5,9},{9,13},{2,6},{6,10},{10,14},{3,7},{... | collective-permute-start | bytes 98312 | tf_op jit(solution)/shard_map/ppermute | solution.py:22
  88.7 0.6 copy.19
  89.3 0.6 dynamic_slice.12.count_ref
  89.9 18.7 %collective-permute-done.7 = bf16[2,8192]{1,0:T(2,128)(2,1)S(1)} collective-permute-done((bf16[2,8192]{1,0:T(2,128)(2,1)S(1)}, bf16[2,8192]{1,0:T(2,128)(2,1)S(1)}, u32[]{:S(2)}, u32[]{:S(2)}) %collective-permute-start.7) | collective-permute-done | bytes 32800 | tf_op jit(solution)/shard_map/ppermute | solution.py:23
  108.6 0.7 maximum_convert_fusion.info_ref
  109.3 1.0 copy-done.2
  110.7 53.3 %shard_map.105 = bf16[32,64,64]{2,1,0:T(8,128)(2,1)} custom-call(s32[32]{0:T(128)} %dynamic_slice.12.count_ref, s32[16384]{0:T(1024)} %bitcast.32, bf16[64,8192]{1,0:T(8,128)(2,1)} %copy-done.2, bf16[64,8192]{1,0:T(8,128)(2,1)} %shard_map.104.own_ref, bf16[64,8192]{1,0:T(8,128)(2,1)} %copy-done.3, f32[2,192,128]{2,1,0:T(8,128)} %maximum_convert_fusion.info_ref), custom_call_target="tpu_custom_call" | custom-call | flops 1000000000 | bytes 4194304 | tf_op jit(solution)/shard_map/pallas_call | solution.py:279
  164.1 4.3 %copy.15 = bf16[256,32,128]{2,1,0:T(8,128)(2,1)} copy(bf16[256,32,128]{2,0,1:T(8,128)(2,1)} %all-gather.8.cloned.1.call-done) | data formatting | bytes 4194304 | tf_op jit(solution)/shard_map/all_gather | solution.py:298
  168.4 18.5 %all-gather.6.cloned.1.call-done = bf16[128,64,64]{2,1,0:T(8,128)(2,1)} async-done(((bf16[32,64,64]{2,1,0:T(8,128)(2,1)}), bf16[128,64,64]{2,1,0:T(8,128)(2,1)}) %all-gather.6.cloned.1.call-update) | async-done | bytes 1048592 | tf_op jit(solution)/shard_map/all_gather | solution.py:293
  186.8 2.3 %constant_dynamic-slice_fusion.1.snap_mix_ref = bf16[128,32,64]{2,1,0:T(8,128)(2,1)} fusion(bf16[128,64,64]{2,1,0:T(8,128)(2,1)} %all-gather.6.cloned.1.call-done, s32[]{:T(128)S(6)} %select_n.11), kind=kLoop, calls=%fused_computation.26 | loop fusion | bytes 1048580 | tf_op jit(solution)/shard_map/dynamic_slice | solution.py:296
  189.1 1.9 constant_dynamic-slice_fusion.field_mix_ref
  191.0 8.8 %shard_map.106 = (bf16[128,32,128]{2,1,0:T(8,128)(2,1)}, bf16[128,16,128]{2,1,0:T(8,128)(2,1)}) custom-call(bf16[2,128,32,128]{3,2,1,0:T(8,128)(2,1)} %bitcast.28, bf16[128,32,64]{2,1,0:T(8,128)(2,1)} %constant_dynamic-slice_fusion.1.snap_mix_ref, bf16[4,128,16,128]{3,2,1,0:T(8,128)(2,1)} %bitcast.27, ...), custom_call_target="tpu_custom_call" | custom-call | flops 100000000 | bytes 4194304 | tf_op jit(solution)/shard_map/pallas_call | solution.py:299
  199.8 2.7 %copy.17 = bf16[1,32,128,128]{3,2,1,0:T(8,128)(2,1)} copy(bf16[1,32,128,128]{3,1,2,0:T(8,128)(2,1)} %bitcast.30) | data formatting | bytes 2097152
  202.5 0.9 copy.18
  (44 shorter events, 1.8 us)
Async XLA Ops:
  7.2 81.5 %copy-start = (s32[128,512]{1,0:T(8,128)S(1)}, s32[128,512]{1,0:T(8,128)}, u32[]{:S(2)}) copy-start(s32[128,512]{1,0:T(8,128)} %param.16) | copy-start | bytes 786436
  7.2 46.0 %all-gather.10.cloned.1.call-start = ((), (), s32[]{:S(2)}) async-start(), calls=%async_computation.2 | async-start | bytes 2621440 | tf_op jit(solution)/shard_map/all_gather | solution.py:263
  8.1 9.1 %collective-permute-start = (f32[16,1,128]{2,1,0:T(1,128)S(1)}, f32[16,1,128]{2,1,0:T(1,128)S(1)}, u32[]{:S(2)}, u32[]{:S(2)}) collective-permute-start(f32[16,1,128]{2,1,0:T(1,128)S(1)} %get-tuple-element.20), channel_id=1, source_target_pairs={{0,4},{4,8},{8,12},{1,5},{5,9},{9,13},{2,6},{6,10},{10,14},{3,7},{... | collective-permute-start | bytes 24584 | tf_op jit(solution)/shard_map/ppermute | solution.py:22
  13.1 3.4 %copy-start.1 = (f32[16,128,128]{2,1,0:T(8,128)S(1)}, f32[16,128,128]{2,1,0:T(8,128)}, u32[]{:S(2)}) copy-start(f32[16,128,128]{2,1,0:T(8,128)} %param.10) | copy-start | bytes 3145732
  13.1 5.7 %collective-permute-start.1 = (f32[16,1,128]{2,1,0:T(1,128)S(1)}, f32[16,1,128]{2,1,0:T(1,128)S(1)}, u32[]{:S(2)}, u32[]{:S(2)}) collective-permute-start(f32[16,1,128]{2,1,0:T(1,128)S(1)} %get-tuple-element.21), channel_id=1, source_target_pairs={{4,0},{8,4},{12,8},{5,1},{9,5},{13,9},{6,2},{10,6},{14,10},{7,3},{... | collective-permute-start | bytes 24584 | tf_op jit(solution)/shard_map/ppermute | solution.py:23
  16.4 0.8 copy-start.8
  16.5 2.3 %copy-start.5 = (f32[128,128]{1,0:T(8,128)S(1)}, f32[128,128]{1,0:T(8,128)}, u32[]{:S(2)}) copy-start(f32[128,128]{1,0:T(8,128)} %param.11) | copy-start | bytes 196612
  19.9 5.2 %collective-permute-start.2 = (f32[16,1,128]{2,1,0:T(1,128)S(1)}, f32[16,1,128]{2,1,0:T(1,128)S(1)}, u32[]{:S(2)}, u32[]{:S(2)}) collective-permute-start(f32[16,1,128]{2,1,0:T(1,128)S(1)} %get-tuple-element.10), channel_id=1, source_target_pairs={{0,4},{4,8},{8,12},{1,5},{5,9},{9,13},{2,6},{6,10},{10,14},{3,7},{... | collective-permute-start | bytes 24584 | tf_op jit(solution)/shard_map/ppermute | solution.py:22
  23.4 5.5 %collective-permute-start.3 = (f32[16,1,128]{2,1,0:T(1,128)S(1)}, f32[16,1,128]{2,1,0:T(1,128)S(1)}, u32[]{:S(2)}, u32[]{:S(2)}) collective-permute-start(f32[16,1,128]{2,1,0:T(1,128)S(1)} %get-tuple-element.11), channel_id=1, source_target_pairs={{4,0},{8,4},{12,8},{5,1},{9,5},{13,9},{6,2},{10,6},{14,10},{7,3},{... | collective-permute-start | bytes 24584 | tf_op jit(solution)/shard_map/ppermute | solution.py:23
  29.0 2.4 %copy-start.6 = (f32[8192]{0:T(1024)S(1)}, f32[8192]{0:T(1024)}, u32[]{:S(2)}) copy-start(f32[8192]{0:T(1024)} %param.14) | copy-start | bytes 98308
  29.0 2.5 %copy-start.7 = (f32[8192]{0:T(1024)S(1)}, f32[8192]{0:T(1024)}, u32[]{:S(2)}) copy-start(f32[8192]{0:T(1024)} %param.15) | copy-start | bytes 98308
  30.6 133.4 %all-gather.8.cloned.1.call-start = ((), (), s32[]{:S(2)}) async-start(), calls=%async_computation.1 | async-start | bytes 3145728 | tf_op jit(solution)/shard_map/all_gather | solution.py:298
  31.4 155.5 %all-gather.6.cloned.1.call-start = ((), (), s32[]{:S(2)}) async-start(), calls=%async_computation | async-start | bytes 2621440 | tf_op jit(solution)/shard_map/all_gather | solution.py:293
  57.5 31.8 %copy-start.9 = (s32[128]{0:T(128)S(1)}, s32[128]{0:T(128)}, u32[]{:S(2)}) copy-start(s32[128]{0:T(128)} %param.17) | copy-start | bytes 1540
  77.3 32.0 %collective-permute-start.4 = (bf16[64,8192]{1,0:T(8,128)(2,1)}, bf16[64,8192]{1,0:T(8,128)(2,1)S(1)}, u32[]{:S(2)}, u32[]{:S(2)}) collective-permute-start(bf16[64,8192]{1,0:T(8,128)(2,1)} %shard_map.104.own_ref), channel_id=1, source_target_pairs={{0,4},{4,8},{8,12},{1,5},{5,9},{9,13},{2,6},{6,10},{10,14},{3,7},{... | collective-permute-start | bytes 3145736 | tf_op jit(solution)/shard_map/ppermute | solution.py:240
  80.8 28.6 %collective-permute-start.5 = (bf16[64,8192]{1,0:T(8,128)(2,1)}, bf16[64,8192]{1,0:T(8,128)(2,1)S(1)}, u32[]{:S(2)}, u32[]{:S(2)}) collective-permute-start(bf16[64,8192]{1,0:T(8,128)(2,1)} %shard_map.104.own_ref), channel_id=1, source_target_pairs={{4,0},{8,4},{12,8},{5,1},{9,5},{13,9},{6,2},{10,6},{14,10},{7,3},{... | collective-permute-start | bytes 3145736 | tf_op jit(solution)/shard_map/ppermute | solution.py:241
  82.2 26.4 %collective-permute-start.7 = (bf16[2,8192]{1,0:T(2,128)(2,1)S(1)}, bf16[2,8192]{1,0:T(2,128)(2,1)S(1)}, u32[]{:S(2)}, u32[]{:S(2)}) collective-permute-start(bf16[2,8192]{1,0:T(2,128)(2,1)S(1)} %pad_maximum_fusion.4), channel_id=1, source_target_pairs={{4,0},{8,4},{12,8},{5,1},{9,5},{13,9},{6,2},{10,6},{14,10},{7,3},{... | collective-permute-start | bytes 98312 | tf_op jit(solution)/shard_map/ppermute | solution.py:23
  83.5 25.2 %collective-permute-start.6 = (bf16[2,8192]{1,0:T(2,128)(2,1)S(1)}, bf16[2,8192]{1,0:T(2,128)(2,1)S(1)}, u32[]{:S(2)}, u32[]{:S(2)}) collective-permute-start(bf16[2,8192]{1,0:T(2,128)(2,1)S(1)} %pad_maximum_fusion.4), channel_id=1, source_target_pairs={{0,4},{4,8},{8,12},{1,5},{5,9},{9,13},{2,6},{6,10},{10,14},{3,7},{... | collective-permute-start | bytes 98312 | tf_op jit(solution)/shard_map/ppermute | solution.py:22
  109.3 1.0 copy-start.2
  109.3 1.4 copy-start.3
  199.8 2.7 %copy-start.4 = (bf16[128,16,128]{2,1,0:T(8,128)(2,1)S(1)}, bf16[128,16,128]{2,1,0:T(8,128)(2,1)}, u32[]{:S(2)}) copy-start(bf16[128,16,128]{2,1,0:T(8,128)(2,1)} %get-tuple-element.5) | copy-start | bytes 1572868
Sparse Core Ops, SparseCore 0:
  30.7 22.4 all-gather.9
  54.7 10.6 all-gather.7
  164.1 22.6 all-gather.5

commit v2 on v1

--- a/solution.py
+++ b/solution.py
@@ -211,7 +211,8 @@
         weights = root * inv[n] + mean_weight
         mixed = weights + (1.0 - jnp.sum(weights, axis=0, keepdims=True)) * (1.0 / members)
         wide[:, n, :] = mixed.T[:share]
-    out_ref[...] = wide[...].astype(jnp.bfloat16)
+    half = members // 2
+    out_ref[...] = jnp.concatenate([wide[:, :half], wide[:, half:]], axis=2).astype(jnp.bfloat16)
 
 
 def update_kernel(snap_ref, snap_mix_ref, field_ref, field_mix_ref, smooth_ref, analysis_ref):
@@ -233,13 +234,183 @@
     lax.fori_loop(0, tiles, tile, 0, unroll=4)
 
 
-def halo_parts(array, axis, dim, width):
-    size, length = lax.axis_size(axis), array.shape[dim]
-    up = [(i, (i + 1) % size) for i in range(size - 1)]
-    down = [(j, i) for i, j in up]
-    before = lax.ppermute(lax.slice_in_dim(array, length - width, length, axis=dim), axis, up)
-    after = lax.ppermute(lax.slice_in_dim(array, 0, width, axis=dim), axis, down)
-    return before, after
+MESH = pl.DeviceIdType.MESH
+CHUNKS = 4
+
+
+def gather_kernel(block_ref, out_ref, own_sem, send_sem, recv_sem, pass_send, pass_recv):
+    lag, core = lax.axis_index("lag"), lax.axis_index("member")
+    lags = lax.axis_size("lag")
+    size = block_ref.shape[0] // CHUNKS
+    other = {"member": 1 - core}
+    barrier = pltpu.get_barrier_semaphore()
+    for d in range(1, lags):
+        pl.semaphore_signal(
+            barrier, inc=1, device_id={"lag": lax.rem(lag + d, lags)}, device_id_type=MESH
+        )
+    pl.semaphore_signal(barrier, inc=1, device_id=other, device_id_type=MESH)
+    pl.semaphore_wait(barrier, lags)
+    mine = lag * 2 + core
+    keep = pltpu.make_async_copy(block_ref, out_ref.at[mine], own_sem)
+    keep.start()
+    across = []
+    for c in range(CHUNKS):
+        for d in range(1, lags):
+            copy = pltpu.make_async_remote_copy(
+                src_ref=block_ref.at[pl.ds(c * size, size)],
+                dst_ref=out_ref.at[mine, pl.ds(c * size, size)],
+                send_sem=send_sem.at[d, c],
+                recv_sem=recv_sem.at[d, c],
+                device_id={"lag": lax.rem(lag + d, lags)},
+                device_id_type=MESH,
+            )
+            copy.start()
+            across.append((c, d, copy))
+    beside = []
+    for c in range(CHUNKS):
+        copy = pltpu.make_async_remote_copy(
+            src_ref=block_ref.at[pl.ds(c * size, size)],
+            dst_ref=out_ref.at[mine, pl.ds(c * size, size)],
+            send_sem=pass_send.at[0, c],
+            recv_sem=pass_recv.at[0, c],
+            device_id=other,
+            device_id_type=MESH,
+        )
+        copy.start()
+        beside.append(copy)
+    for c, d, copy in across:
+        copy.wait_recv()
+        slot = lax.rem(lag + lags - d, lags) * 2 + core
+        onward = pltpu.make_async_remote_copy(
+            src_ref=out_ref.at[slot, pl.ds(c * size, size)],
+            dst_ref=out_ref.at[slot, pl.ds(c * size, size)],
+            send_sem=pass_send.at[d, c],
+            recv_sem=pass_recv.at[d, c],
+            device_id=other,
+            device_id_type=MESH,
+        )
+        onward.start()
+        beside.append(onward)
+    for c, d, copy in across:
+        copy.wait_send()
+    for copy in beside:
+        copy.wait()
+    keep.wait()
+
+
+def group_gather(block, collective_id):
+    lags = lax.axis_size("lag")
+    sems = pltpu.SemaphoreType.DMA((lags, CHUNKS))
+    return pl.pallas_call(
+        gather_kernel,
+        out_shape=jax.ShapeDtypeStruct((lags * 2,) + block.shape, block.dtype),
+        in_specs=[pl.BlockSpec(memory_space=pl.ANY)],
+        out_specs=pl.BlockSpec(memory_space=pl.ANY),
+        scratch_shapes=[pltpu.SemaphoreType.DMA, sems, sems, sems, sems],
+        compiler_params=pltpu.CompilerParams(collective_id=collective_id, has_side_effects=True),
+    )(block)
+
+
+def halo_kernel(block_ref, before_ref, after_ref, send_sem, recv_sem, pass_send, pass_recv):
+    region, core = lax.axis_index("region"), lax.axis_index("member")
+    regions = lax.axis_size("region")
+    half = block_ref.shape[0] // 2
+    size = half // 2
+    other = {"member": 1 - core}
+    has_before = region > 0
+    has_after = region < regions - 1
+    barrier = pltpu.get_barrier_semaphore()
+    pl.semaphore_signal(barrier, inc=1, device_id=other, device_id_type=MESH)
+
+    @pl.when(has_before)
+    def _():
+        pl.semaphore_signal(
+            barrier, inc=1, device_id={"region": region - 1}, device_id_type=MESH
+        )
+
+    @pl.when(has_after)
+    def _():
+        pl.semaphore_signal(
+            barrier, inc=1, device_id={"region": region + 1}, device_id_type=MESH
+        )
+
+    peers = 1 + has_before.astype(jnp.int32) + has_after.astype(jnp.int32)
+    pl.semaphore_wait(barrier, peers)
+
+    def rows(c):
+        return pl.ds(pl.multiple_of(core * half + c * size, 16), size)
+
+    def to_side(side, c):
+        return pltpu.make_async_remote_copy(
+            src_ref=block_ref.at[rows(c)],
+            dst_ref=(before_ref, after_ref)[side].at[rows(c)],
+            send_sem=send_sem.at[side, c],
+            recv_sem=recv_sem.at[side, c],
+            device_id={"region": region + 1 - 2 * side},
+            device_id_type=MESH,
+        )
+
+    def onward(side, c):
+        ref = (before_ref, after_ref)[side]
+        return pltpu.make_async_remote_copy(
+            src_ref=ref.at[rows(c)],
+            dst_ref=ref.at[rows(c)],
+            send_sem=pass_send.at[side, c],
+            recv_sem=pass_recv.at[side, c],
+            device_id=other,
+            device_id_type=MESH,
+        )
+
+    sends = (has_after, has_before)
+    receives = (has_before, has_after)
+    for side in range(2):
+
+        @pl.when(sends[side])
+        def _(side=side):
+            for c in range(2):
+                to_side(side, c).start()
+
+    for side, ref in enumerate((before_ref, after_ref)):
+
+        @pl.when(jnp.logical_not(receives[side]))
+        def _(ref=ref):
+            ref[...] = jnp.zeros_like(ref)
+
+    for c in range(2):
+        for side in range(2):
+
+            @pl.when(receives[side])
+            def _(side=side, c=c):
+                to_side(side, c).wait_recv()
+                onward(side, c).start()
+
+    for side in range(2):
+
+        @pl.when(sends[side])
+        def _(side=side):
+            for c in range(2):
+                to_side(side, c).wait_send()
+
+        @pl.when(receives[side])
+        def _(side=side):
+            for c in range(2):
+                onward(side, c).wait()
+
+
+def sample_halo(block, collective_id):
+    sems = pltpu.SemaphoreType.DMA((2, 2))
+    vmem = pl.BlockSpec(memory_space=pltpu.VMEM)
+    shape = jax.ShapeDtypeStruct(block.shape, block.dtype)
+    return pl.pallas_call(
+        halo_kernel,
+        out_shape=(shape, shape),
+        in_specs=[vmem],
+        out_specs=(vmem, vmem),
+        scratch_shapes=[sems, sems, sems, sems],
+        compiler_params=pltpu.CompilerParams(
+            collective_id=collective_id, has_side_effects=True, vmem_limit_bytes=VMEM_BYTES
+        ),
+    )(block)
 
 
 def local(
@@ -260,7 +431,7 @@
     group_size = lax.axis_size(("lag", "member"))
     group_rank = lax.axis_index(("lag", "member"))
     by_row = newest.transpose(1, 0, 2)
-    everyone = lax.all_gather(by_row, ("lag", "member"), axis=0)
+    everyone = group_gather(by_row, 1)
     members = group_size * own_members
     vmem, smem = pltpu.VMEM, pltpu.SMEM
     rows, cols = newest.shape[1:]
@@ -271,14 +442,14 @@
         (smem, vmem),
         10**8,
     )(obs_cell, everyone)
-    before, after = halo_parts(sampled, "region", 1, obs_count)
+    before, after = sample_halo(sampled, 2)
     share = tile_obs.shape[0] // group_size
     first_tile = group_rank * share
     my_index = lax.dynamic_slice_in_dim(tile_obs, first_tile, share, 0).reshape(-1)
     my_count = lax.dynamic_slice_in_dim(tile_count, first_tile, share, 0)
     mine = vmem_call(
         mixing_kernel,
-        jax.ShapeDtypeStruct((share, members, members), jnp.bfloat16),
+        jax.ShapeDtypeStruct((share, members // 2, 2 * members), jnp.bfloat16),
         [
             pltpu.VMEM((3 * obs_count, LANES), jnp.float32),
             pltpu.VMEM((tile_obs.shape[1], LANES), jnp.float32),
@@ -290,11 +461,17 @@
         (smem, smem, vmem, vmem, vmem, vmem),
         10**9,
     )(my_count, my_index, before, sampled, after, window_info.reshape(2, -1, LANES))
-    mixing = lax.all_gather(mine, ("lag", "member"), axis=0, tiled=True)
+    mixing = group_gather(mine, 3)
+    mixing = mixing.reshape(-1, members // 2, 2 * members)
     member_rank = lax.axis_index("member")
     half_members = snapshots.shape[1]
-    snap_mix = lax.dynamic_slice_in_dim(mixing, member_rank * half_members, half_members, 1)
-    field_mix = lax.dynamic_slice_in_dim(mixing, group_rank * own_members, own_members, 1)
+    snap_mix = lax.dynamic_slice_in_dim(mixing, member_rank * members, members, 2)
+    first_member = group_rank * own_members
+    field_mix = lax.dynamic_slice(
+        mixing,
+        (0, first_member % half_members, first_member // half_members * members),
+        (mixing.shape[0], own_members, members),
+    )
     snaps = lax.all_gather(snapshots[0].transpose(1, 0, 2), "member", axis=0)
     smoothed, analysis = vmem_call(
         update_kernel,

time: 211 us -> 199 us (0.943)
  waiting for transfers between devices: 64.9 us -> 3.57 us
  Pallas kernels: 81.9 us -> 129 us
  other arithmetic: 3.19 us -> 8.45 us
  starting transfers between devices: 22.4 us -> 18.6 us
    pallas_call x1 -> x4, Pallas kernels: 53.3 us -> 100 us  [the longest x1 49.9 us: local(): vmem_call(mixing_kernel, jax.ShapeDtypeStruct((share, members // 2, 2 * m...]
    all_gather x2 -> x0, waiting for transfers between devices: 40.2 us -> none  [the longest x1 21.7 us: local(): everyone = lax.all_gather(by_row, ('lag', 'member'), axis=0)]
    ppermute x3, waiting for transfers between devices: 24 us -> 3.54 us  [with_halo(): after = lax.ppermute(leading, axis, down)]
    ppermute x2 -> x0, starting transfers between devices: 4.73 us -> none  [the longest x1 3.44 us: halo_parts(): lax.ppermute(lax.slice_in_dim(array, length - width, length, axis=dim), a...]
    all_gather x1 -> x0, local copies, waits for them, and re-layouts: 4.3 us -> none  [local(): everyone = lax.all_gather(by_row, ('lag', 'member'), axis=0)]
    unnamed x26 -> x19, local copies, waits for them, and re-layouts: 6.13 us -> 9.11 us
  transfers between devices with their start and end apart: 11 -> 7, of which waited for: 5 -> 1; matrix products, arithmetic and copies ran while one was open for 6% -> 11% of each run, Pallas kernels for 35% -> 61%
where the time goes in v2:
time: 199 us; the launch traced here: 197 us
  Pallas kernels  129 us (65%)
  local copies, waits for them, and re-layouts  22.7 us (11%)
  starting transfers between devices  18.6 us (9%)
  between operations  14.2 us (7%)
  other arithmetic  8.45 us (4%)
  waiting for transfers between devices  3.57 us (2%)
    pallas_call x1, Pallas kernels, local(): vmem_call(mixing_kernel, jax.ShapeDtypeStruct((share, members // 2, 2 * m...  49.9 us
    pallas_call x2, Pallas kernels, group_gather(): pl.pallas_call(gather_kernel, out_shape=jax.ShapeDtypeStruct((lags * 2,)...  32.5 us
    pallas_call x1, Pallas kernels, local(): vmem_call(sample_kernel, jax.ShapeDtypeStruct((members, obs_count), jnp.b...  19.8 us
    pallas_call x1, Pallas kernels, sample_halo(): pl.pallas_call(halo_kernel, out_shape=(shape, shape), in_specs=[vmem], ou...  18.1 us
    ppermute x3, starting transfers between devices, with_halo(): before = lax.ppermute(last, axis, up)  14.7 us
    unnamed x19, local copies, waits for them, and re-layouts  9.11 us
    pallas_call x1, Pallas kernels, local(): vmem_call(update_kernel, (jax.ShapeDtypeStruct((rows, half_members, cols)...  8.86 us
    all_gather x1, local copies, waits for them, and re-layouts, local(): snaps = lax.all_gather(snapshots[0].transpose(1, 0, 2), 'member', axis=0)  4.29 us
  transfers between devices with their start and end apart: 7, of which 1 were waited for; matrix products, arithmetic and copies ran while one was open for 11% of the time, Pallas kernels for 61%

profile of v2, /device:TPU:0, one launch (start us, length us, event | category | flops | bytes accessed | tf_op | source)
XLA Modules:
  0.0 196.5 jit_solution(13152336642728994727)
XLA Ops:
  7.2 0.8 convert.12
  8.0 0.8 convert.13
  8.8 0.7 pad_maximum_fusion.4
  9.5 1.3 collective-permute-start.5
  10.8 6.2 %collective-permute-start.4 = (bf16[2,8192]{1,0:T(2,128)(2,1)}, bf16[2,8192]{1,0:T(2,128)(2,1)}, u32[]{:S(2)}, u32[]{:S(2)}) collective-permute-start(bf16[2,8192]{1,0:T(2,128)(2,1)} %pad_maximum_fusion.4), channel_id=1, source_target_pairs={{0,4},{4,8},{8,12},{1,5},{5,9},{9,13},{2,6},{6,10},{10,14},{3,7},{... | collective-permute-start | bytes 98312 | tf_op jit(solution)/shard_map/ppermute | solution.py:22
  17.0 1.8 copy.21
  19.4 3.9 %collective-permute-start = (f32[16,1,128]{2,0,1:T(8,128)}, f32[16,1,128]{2,0,1:T(8,128)}, u32[]{:S(2)}, u32[]{:S(2)}) collective-permute-start(f32[16,1,128]{2,0,1:T(8,128)} %get-tuple-element.22), channel_id=1, source_target_pairs={{0,4},{4,8},{8,12},{1,5},{5,9},{9,13},{2,6},{6,10},{10,14},{3,7},{... | collective-permute-start | bytes 24584 | tf_op jit(solution)/shard_map/ppermute | solution.py:22
  23.3 1.3 collective-permute-start.1
  25.0 1.7 fusion.20
  27.3 0.6 dynamic-slice_bitcast_fusion
  27.9 0.8 convert_element_type.12
  28.8 1.5 copy.24
  30.3 1.3 dynamic_slice.12.count_ref
  31.5 2.4 %fusion.14 = f32[16,128,128]{2,0,1:T(8,128)S(1)} fusion(f32[16,128,128]{2,0,1:T(8,128)S(1)} %copy.21, f32[16,1,128]{2,0,1:T(8,128)} %collective-permute-done.1, f32[16,1,128]{2,0,1:T(8,128)} %collective-permute-done, f32[16,128,127]{2,0,1:T(8,128)S(1)} %get-tuple-element.19, f32[16,128,1]{2,0,1:T(8,128)} %get-tuple-element.21, ...), kind=kLoop, calls=%fused_computation.17 | loop fusion | flops 3145728 | bytes 4341760 | tf_op jit(solution)/shard_map/mul | solution.py:34
  34.0 4.6 %collective-permute-start.2 = (f32[16,1,128]{2,0,1:T(8,128)S(1)}, f32[16,1,128]{2,0,1:T(8,128)S(1)}, u32[]{:S(2)}, u32[]{:S(2)}) collective-permute-start(f32[16,1,128]{2,0,1:T(8,128)S(1)} %get-tuple-element.12), channel_id=1, source_target_pairs={{0,4},{4,8},{8,12},{1,5},{5,9},{9,13},{2,6},{6,10},{10,14},{3,7},{... | collective-permute-start | bytes 24584 | tf_op jit(solution)/shard_map/ppermute | solution.py:22
  38.6 1.3 collective-permute-start.3
  40.6 3.5 %collective-permute-done.3 = f32[16,1,128]{2,0,1:T(8,128)S(1)} collective-permute-done((f32[16,1,128]{2,0,1:T(8,128)S(1)}, f32[16,1,128]{2,0,1:T(8,128)S(1)}, u32[]{:S(2)}, u32[]{:S(2)}) %collective-permute-start.3) | collective-permute-done | bytes 8224 | tf_op jit(solution)/shard_map/ppermute | solution.py:23
  44.1 1.7 fusion.15.block_ref
  45.8 18.8 %shard_map.104.field_ref = bf16[4,128,16,128]{3,2,1,0:T(8,128)(2,1)} custom-call(bf16[128,16,128]{2,1,0:T(8,128)(2,1)} %fusion.15.block_ref), custom_call_target="tpu_custom_call" | custom-call | tf_op jit(solution)/shard_map/pallas_call | solution.py:304
  64.6 19.8 %shard_map.105.block_ref.own_ref = bf16[64,8192]{1,0:T(8,128)(2,1)} custom-call(s32[8192]{0:T(1024)} %cell_ref.1, bf16[4,128,16,128]{3,2,1,0:T(8,128)(2,1)} %shard_map.104.field_ref), custom_call_target="tpu_custom_call" | custom-call | flops 100000000 | bytes 4194304 | tf_op jit(solution)/shard_map/pallas_call | solution.py:438
  84.4 18.1 %shard_map.106 = (bf16[64,8192]{1,0:T(8,128)(2,1)}, bf16[64,8192]{1,0:T(8,128)(2,1)}) custom-call(bf16[64,8192]{1,0:T(8,128)(2,1)} %shard_map.105.block_ref.own_ref), custom_call_target="tpu_custom_call" | custom-call | tf_op jit(solution)/shard_map/pallas_call | solution.py:404
  102.5 0.8 copy.29
  103.2 0.8 copy.30
  104.0 0.7 maximum_convert_fusion.info_ref
  104.7 49.9 %shard_map.107.block_ref = bf16[32,32,128]{2,1,0:T(8,128)(2,1)} custom-call(s32[32]{0:T(128)} %dynamic_slice.12.count_ref, s32[16384]{0:T(1024)} %bitcast.34, bf16[64,8192]{1,0:T(8,128)(2,1)} %get-tuple-element.6.before_ref, bf16[64,8192]{1,0:T(8,128)(2,1)} %shard_map.105.block_ref.own_ref, bf16[64,8192]{1,0:T(8,128)(2,1)} %get-tuple-element.7.after_ref, ...), custom_call_target="tpu_custom_call" | custom-call | flops 1000000000 | bytes 4194304 | tf_op jit(solution)/shard_map/pallas_call | solution.py:450
  154.6 13.7 %shard_map.108 = bf16[4,32,32,128]{3,2,1,0:T(8,128)(2,1)} custom-call(bf16[32,32,128]{2,1,0:T(8,128)(2,1)} %shard_map.107.block_ref), custom_call_target="tpu_custom_call" | custom-call | tf_op jit(solution)/shard_map/pallas_call | solution.py:304
  168.2 2.1 %constant_dynamic-slice_fusion.field_mix_ref = bf16[128,16,64]{2,1,0:T(8,128)(2,1)} fusion(bf16[128,32,128]{2,1,0:T(8,128)(2,1)} %bitcast.27, s32[]{:T(128)S(6)} %select_n.27, s32[]{:T(128)S(6)} %select_n.29), kind=kLoop, calls=%fused_computation.25 | loop fusion | bytes 524296 | tf_op jit(solution)/shard_map/dynamic_slice | solution.py:470
  170.4 2.5 %constant_dynamic-slice_fusion.1.snap_mix_ref = bf16[128,32,64]{2,1,0:T(8,128)(2,1)} fusion(bf16[128,32,128]{2,1,0:T(8,128)(2,1)} %bitcast.28, s32[]{:T(128)S(6)} %select_n.25), kind=kLoop, calls=%fused_computation.26 | loop fusion | bytes 1048580 | tf_op jit(solution)/shard_map/dynamic_slice | solution.py:468
  172.9 4.3 %copy.11 = bf16[256,32,128]{2,1,0:T(8,128)(2,1)} copy(bf16[256,32,128]{2,0,1:T(8,128)(2,1)} %all-gather.3.cloned.1.call-done) | data formatting | bytes 4194304 | tf_op jit(solution)/shard_map/all_gather | solution.py:475
  177.2 8.9 %shard_map.109 = (bf16[128,32,128]{2,1,0:T(8,128)(2,1)}, bf16[128,16,128]{2,1,0:T(8,128)(2,1)}) custom-call(bf16[2,128,32,128]{3,2,1,0:T(8,128)(2,1)} %bitcast.26, bf16[128,32,64]{2,1,0:T(8,128)(2,1)} %constant_dynamic-slice_fusion.1.snap_mix_ref, bf16[4,128,16,128]{3,2,1,0:T(8,128)(2,1)} %shard_map.104.field_ref, ...), custom_call_target="tpu_custom_call" | custom-call | flops 100000000 | bytes 4194304 | tf_op jit(solution)/shard_map/pallas_call | solution.py:476
  186.1 2.7 %copy.22 = bf16[1,32,128,128]{3,2,1,0:T(8,128)(2,1)} copy(bf16[1,32,128,128]{3,1,2,0:T(8,128)(2,1)} %bitcast.30) | data formatting | bytes 2097152
  188.8 0.9 copy.23
  (29 shorter events, 2.4 us)
Async XLA Ops:
  7.2 20.1 %copy-start = (s32[128,512]{1,0:T(8,128)S(1)}, s32[128,512]{1,0:T(8,128)}, u32[]{:S(2)}) copy-start(s32[128,512]{1,0:T(8,128)} %param.16) | copy-start | bytes 786436
  7.2 165.8 %all-gather.3.cloned.1.call-start = ((), (), s32[]{:S(2)}) async-start(), calls=%async_computation | async-start | bytes 3145728 | tf_op jit(solution)/shard_map/all_gather | solution.py:475
  9.5 92.9 %collective-permute-start.5 = (bf16[2,8192]{1,0:T(2,128)(2,1)}, bf16[2,8192]{1,0:T(2,128)(2,1)}, u32[]{:S(2)}, u32[]{:S(2)}) collective-permute-start(bf16[2,8192]{1,0:T(2,128)(2,1)} %pad_maximum_fusion.4), channel_id=1, source_target_pairs={{4,0},{8,4},{12,8},{5,1},{9,5},{13,9},{6,2},{10,6},{14,10},{7,3},{... | collective-permute-start | bytes 98312 | tf_op jit(solution)/shard_map/ppermute | solution.py:23
  10.8 92.4 %collective-permute-start.4 = (bf16[2,8192]{1,0:T(2,128)(2,1)}, bf16[2,8192]{1,0:T(2,128)(2,1)}, u32[]{:S(2)}, u32[]{:S(2)}) collective-permute-start(bf16[2,8192]{1,0:T(2,128)(2,1)} %pad_maximum_fusion.4), channel_id=1, source_target_pairs={{0,4},{4,8},{8,12},{1,5},{5,9},{9,13},{2,6},{6,10},{10,14},{3,7},{... | collective-permute-start | bytes 98312 | tf_op jit(solution)/shard_map/ppermute | solution.py:22
  19.4 12.1 %collective-permute-start = (f32[16,1,128]{2,0,1:T(8,128)}, f32[16,1,128]{2,0,1:T(8,128)}, u32[]{:S(2)}, u32[]{:S(2)}) collective-permute-start(f32[16,1,128]{2,0,1:T(8,128)} %get-tuple-element.22), channel_id=1, source_target_pairs={{0,4},{4,8},{8,12},{1,5},{5,9},{9,13},{2,6},{6,10},{10,14},{3,7},{... | collective-permute-start | bytes 24584 | tf_op jit(solution)/shard_map/ppermute | solution.py:22
  23.3 8.2 %collective-permute-start.1 = (f32[16,1,128]{2,0,1:T(8,128)}, f32[16,1,128]{2,0,1:T(8,128)}, u32[]{:S(2)}, u32[]{:S(2)}) collective-permute-start(f32[16,1,128]{2,0,1:T(8,128)} %get-tuple-element.23), channel_id=1, source_target_pairs={{4,0},{8,4},{12,8},{5,1},{9,5},{13,9},{6,2},{10,6},{14,10},{7,3},{... | collective-permute-start | bytes 24584 | tf_op jit(solution)/shard_map/ppermute | solution.py:23
  25.0 1.7 copy-start.3
  25.0 1.7 copy-start.4
  25.0 6.5 %copy-start.2 = (f32[128,128]{1,0:T(8,128)S(1)}, f32[128,128]{1,0:T(8,128)}, u32[]{:S(2)}) copy-start(f32[128,128]{1,0:T(8,128)} %param.11) | copy-start | bytes 196612
  34.0 6.6 %collective-permute-start.2 = (f32[16,1,128]{2,0,1:T(8,128)S(1)}, f32[16,1,128]{2,0,1:T(8,128)S(1)}, u32[]{:S(2)}, u32[]{:S(2)}) collective-permute-start(f32[16,1,128]{2,0,1:T(8,128)S(1)} %get-tuple-element.12), channel_id=1, source_target_pairs={{0,4},{4,8},{8,12},{1,5},{5,9},{9,13},{2,6},{6,10},{10,14},{3,7},{... | collective-permute-start | bytes 24584 | tf_op jit(solution)/shard_map/ppermute | solution.py:22
  38.6 5.5 %collective-permute-start.3 = (f32[16,1,128]{2,0,1:T(8,128)S(1)}, f32[16,1,128]{2,0,1:T(8,128)S(1)}, u32[]{:S(2)}, u32[]{:S(2)}) collective-permute-start(f32[16,1,128]{2,0,1:T(8,128)S(1)} %get-tuple-element.13), channel_id=1, source_target_pairs={{4,0},{8,4},{12,8},{5,1},{9,5},{13,9},{6,2},{10,6},{14,10},{7,3},{... | collective-permute-start | bytes 24584 | tf_op jit(solution)/shard_map/ppermute | solution.py:23
  64.5 39.4 %copy-start.5 = (bf16[1,64,128]{2,1,0:T(8,128)(2,1)S(1)}, bf16[1,64,128]{2,1,0:T(8,128)(2,1)}, u32[]{:S(2)}) copy-start(bf16[1,64,128]{2,1,0:T(8,128)(2,1)} %convert_bitcast_fusion.1) | copy-start | bytes 49156
  186.1 2.7 %copy-start.1 = (bf16[128,16,128]{2,1,0:T(8,128)(2,1)S(1)}, bf16[128,16,128]{2,1,0:T(8,128)(2,1)}, u32[]{:S(2)}) copy-start(bf16[128,16,128]{2,1,0:T(8,128)(2,1)} %get-tuple-element.9) | copy-start | bytes 1572868
Sparse Core Ops, SparseCore 0:
  24.8 11.9 all-gather.2

commit v3 on v2

--- a/solution.py
+++ b/solution.py
@@ -10,19 +10,6 @@
 STEPS = 2
 LANES = 128
 VMEM_BYTES = 56 * 1024 * 1024
-
-
-def with_halo(array, sides, width):
-    for axis, dim in sides:
-        size, length = (lax.axis_size(axis), array.shape[dim])
-        up = [(i, (i + 1) % size) for i in range(size - 1)]
-        down = [(j, i) for i, j in up]
-        last = lax.slice_in_dim(array, length - width, length, axis=dim)
-        leading = lax.slice_in_dim(array, 0, width, axis=dim)
-        before = lax.ppermute(last, axis, up)
-        after = lax.ppermute(leading, axis, down)
-        array = jnp.concatenate([before, array, after], axis=dim)
-    return array
 
 
 def relax(padded, diffusion, sea_mask):
@@ -77,9 +64,11 @@
         base = pl.multiple_of(b * LANES, LANES)
 
         def rows16(g, inner):
+            found = [
+                table[pl.ds(cell_ref[base + g * 16 + q], 1), :members] for q in range(16)
+            ]
             for q in range(16):
-                k = g * 16 + q
-                picked[pl.ds(k, 1), :members] = table[pl.ds(cell_ref[base + k], 1), :members]
+                picked[pl.ds(g * 16 + q, 1), :members] = found[q]
             return inner
 
         lax.fori_loop(0, LANES // 16, rows16, 0, unroll=True)
@@ -122,9 +111,9 @@
         first = t * entries
 
         def rows16(g, inner):
+            found = [table[pl.ds(index_ref[first + g * 16 + q], 1), :] for q in range(16)]
             for q in range(16):
-                k = g * 16 + q
-                picked[pl.ds(k, 1), :] = table[pl.ds(index_ref[first + k], 1), :]
+                picked[pl.ds(g * 16 + q, 1), :] = found[q]
             return inner
 
         lax.fori_loop(0, (count + 15) // 16, rows16, 0)
@@ -146,12 +135,10 @@
 
     lax.fori_loop(0, share, tile, 0)
 
-    copies = LANES // share
-
     def in_lanes(m):
-        return jnp.concatenate([gram[:, m, :]] * copies, axis=0).T[:members]
-
-    row_id = lax.broadcasted_iota(jnp.int32, (members, LANES), 0)
+        return gram[:, m, :].T[:members]
+
+    row_id = lax.broadcasted_iota(jnp.int32, (members, share), 0)
     for m in range(members):
         chol[m] = in_lanes(m) + jnp.where(row_id == m, members - 1.0, 0.0)
     rhs = in_lanes(members)
@@ -168,7 +155,7 @@
                 for q in range(width)
             )
 
-        columns = list(lax.fori_loop(0, p * width, eliminate, tuple(columns)))
+        columns = list(lax.fori_loop(0, p * width, eliminate, tuple(columns), unroll=4))
         for q in range(width):
             at = p * width + q - low
             columns[q] = columns[q] * lax.rsqrt(columns[q][at : at + 1])
@@ -190,7 +177,7 @@
                 rows[q] - solved * group[at + q : at + q + 1] for q in range(width)
             )
 
-        rows = list(lax.fori_loop(0, p * width, substitute, tuple(rows)))
+        rows = list(lax.fori_loop(0, p * width, substitute, tuple(rows), unroll=4))
         for q in range(width):
             n = p * width + q
             rows[q] = rows[q] / chol[n, n : n + 1, :]
@@ -199,18 +186,18 @@
                 rows[later] = rows[later] - rows[q] * chol[n, spot : spot + 1, :]
             inv[n, :high, :] = rows[q]
             if high < members:
-                inv[n, high:, :] = jnp.zeros((members - high, LANES), jnp.float32)
+                inv[n, high:, :] = jnp.zeros((members - high, share), jnp.float32)
 
     def apply(n, mean_weight):
         solved = inv[n]
         return mean_weight + solved * jnp.sum(solved * rhs, axis=0, keepdims=True)
 
-    mean_weight = lax.fori_loop(0, members, apply, jnp.zeros((members, LANES), jnp.float32))
+    mean_weight = lax.fori_loop(0, members, apply, jnp.zeros((members, share), jnp.float32))
     root = float(members - 1) ** 0.5
     for n in range(members):
         weights = root * inv[n] + mean_weight
         mixed = weights + (1.0 - jnp.sum(weights, axis=0, keepdims=True)) * (1.0 / members)
-        wide[:, n, :] = mixed.T[:share]
+        wide[:, n, :] = mixed.T
     half = members // 2
     out_ref[...] = jnp.concatenate([wide[:, :half], wide[:, half:]], axis=2).astype(jnp.bfloat16)
 
@@ -417,24 +404,51 @@
     snapshots, current, diffusivity, landmask, obs_cell, obs_value, obs_weight, tile_obs, tile_count
 ):
     sea_mask = landmask.astype(jnp.float32)
-    field_now = current
-    for substep in range(STEPS):
-        padded = with_halo(field_now, (("region", 1),), 1)
-        field_now = relax(padded, diffusivity, sea_mask)
+    own_members, rows, cols = current.shape
+    depth = STEPS
+
+    def edge(low, margin):
+        return jnp.concatenate(
+            [
+                current[:, low : low + depth].reshape(-1),
+                diffusivity[margin : margin + depth - 1].reshape(-1),
+                sea_mask[margin : margin + depth - 1].reshape(-1),
+                obs_value,
+                obs_weight,
+            ]
+        ).reshape(-1, cols)
+
+    size = lax.axis_size("region")
+    up = [(i, i + 1) for i in range(size - 1)]
+    down = [(j, i) for i, j in up]
+    before = lax.ppermute(edge(rows - depth, rows - depth + 1), "region", up)
+    after = lax.ppermute(edge(0, 0), "region", down)
+    cut = own_members * depth
+    pieces = [
+        (
+            part[:cut].reshape(own_members, depth, cols),
+            part[cut : cut + depth - 1],
+            part[cut + depth - 1 : cut + 2 * (depth - 1)],
+            part[cut + 2 * (depth - 1) :].reshape(2, -1, cols),
+        )
+        for part in (before, after)
+    ]
+    field_now = jnp.concatenate([pieces[0][0], current, pieces[1][0]], axis=1)
+    diffusion = jnp.concatenate([pieces[0][1], diffusivity, pieces[1][1]], axis=0)
+    wide_mask = jnp.concatenate([pieces[0][2], sea_mask, pieces[1][2]], axis=0)
+    for substep in range(depth):
+        span = slice(substep, diffusion.shape[0] - substep)
+        field_now = relax(field_now, diffusion[span], wide_mask[span])
     newest = field_now.astype(jnp.bfloat16)
-    own_members = newest.shape[0]
     obs_count = obs_cell.shape[0]
-    obs_info = jnp.stack([obs_value, obs_weight])
-    window_info = with_halo(obs_info.astype(jnp.bfloat16), (("region", 1),), obs_count).astype(
-        obs_info.dtype
-    )
+    own_info = jnp.stack([obs_value, obs_weight]).reshape(2, -1, cols)
+    window_info = jnp.concatenate([pieces[0][3], own_info, pieces[1][3]], axis=1)
     group_size = lax.axis_size(("lag", "member"))
     group_rank = lax.axis_index(("lag", "member"))
     by_row = newest.transpose(1, 0, 2)
     everyone = group_gather(by_row, 1)
     members = group_size * own_members
     vmem, smem = pltpu.VMEM, pltpu.SMEM
-    rows, cols = newest.shape[1:]
     sampled = vmem_call(
         sample_kernel,
         jax.ShapeDtypeStruct((members, obs_count), jnp.bfloat16),
@@ -454,13 +468,13 @@
             pltpu.VMEM((3 * obs_count, LANES), jnp.float32),
             pltpu.VMEM((tile_obs.shape[1], LANES), jnp.float32),
             pltpu.VMEM((share, LANES, LANES), jnp.float32),
-            pltpu.VMEM((members, members, LANES), jnp.float32),
-            pltpu.VMEM((members, members, LANES), jnp.float32),
+            pltpu.VMEM((members, members, share), jnp.float32),
+            pltpu.VMEM((members, members, share), jnp.float32),
             pltpu.VMEM((share, members, members), jnp.float32),
         ],
         (smem, smem, vmem, vmem, vmem, vmem),
         10**9,
-    )(my_count, my_index, before, sampled, after, window_info.reshape(2, -1, LANES))
+    )(my_count, my_index, before, sampled, after, window_info)
     mixing = group_gather(mine, 3)
     mixing = mixing.reshape(-1, members // 2, 2 * members)
     member_rank = lax.axis_index("member")

time: 199 us -> 170 us (0.85)
  starting transfers between devices: 18.6 us -> 6.26 us
  Pallas kernels: 129 us -> 121 us
  other arithmetic: 8.45 us -> 3.98 us
  local copies, waits for them, and re-layouts: 22.7 us -> 18.5 us
    ppermute x6 -> x2, starting transfers between devices: 18.5 us -> 6.22 us  [the longest x1 4.93 us: local(): before = lax.ppermute(edge(rows - depth, rows - depth + 1), 'region', up)]
    pallas_call x2, Pallas kernels: 32.5 us -> 28.1 us  [group_gather(): pl.pallas_call(gather_kernel, out_shape=jax.ShapeDtypeStruct((lags * 2,)...]
    pallas_call x1, Pallas kernels: 49.9 us -> 45.7 us  [local(): vmem_call(mixing_kernel, jax.ShapeDtypeStruct((share, members // 2, 2 * m...]
    another operation x5 -> x0, other arithmetic: 2.86 us -> none
    unnamed x19 -> x26, local copies, waits for them, and re-layouts: 9.11 us -> 6.86 us
  transfers between devices with their start and end apart: 7 -> 3, of which waited for: 1 -> 1; matrix products, arithmetic and copies ran while one was open for 11% -> 6% of each run, Pallas kernels for 61% -> 67%
where the time goes in v3:
time: 170 us; the launch traced here: 167 us
  Pallas kernels  121 us (71%)
  local copies, waits for them, and re-layouts  18.5 us (11%)
  between operations  14.3 us (8%)
  starting transfers between devices  6.26 us (4%)
  other arithmetic  3.98 us (2%)
  waiting for transfers between devices  3.08 us (2%)
    pallas_call x1, Pallas kernels, local(): vmem_call(mixing_kernel, jax.ShapeDtypeStruct((share, members // 2, 2 * m...  45.7 us
    pallas_call x2, Pallas kernels, group_gather(): pl.pallas_call(gather_kernel, out_shape=jax.ShapeDtypeStruct((lags * 2,)...  28.1 us
    pallas_call x1, Pallas kernels, local(): vmem_call(sample_kernel, jax.ShapeDtypeStruct((members, obs_count), jnp.b...  19.8 us
    pallas_call x1, Pallas kernels, sample_halo(): pl.pallas_call(halo_kernel, out_shape=(shape, shape), in_specs=[vmem], ou...  18.1 us
    pallas_call x1, Pallas kernels, local(): vmem_call(update_kernel, (jax.ShapeDtypeStruct((rows, half_members, cols)...  8.88 us
    unnamed x26, local copies, waits for them, and re-layouts  6.86 us
    ppermute x1, starting transfers between devices, local(): before = lax.ppermute(edge(rows - depth, rows - depth + 1), 'region', up)  4.93 us
    all_gather x1, local copies, waits for them, and re-layouts, local(): snaps = lax.all_gather(snapshots[0].transpose(1, 0, 2), 'member', axis=0)  4.31 us
  transfers between devices with their start and end apart: 3, of which 1 were waited for; matrix products, arithmetic and copies ran while one was open for 6% of the time, Pallas kernels for 67%

profile of v3, /device:TPU:0, one launch (start us, length us, event | category | flops | bytes accessed | tf_op | source)
XLA Modules:
  0.0 166.7 jit_solution(8500659445980927326)
XLA Ops:
  7.2 0.0 all-gather.3.cloned.1.call-start
  7.2 1.0 fusion.18
  8.2 0.8 convert_element_type.6
  9.1 0.7 constant_dynamic-update-slice_fusion.12
  9.8 0.8 constant_dynamic-update-slice_fusion.8
  10.6 0.8 constant_dynamic-update-slice_fusion.6
  11.4 4.9 %collective-permute-start = (f32[162,128]{1,0:T(8,128)S(1)}, f32[162,128]{1,0:T(8,128)S(1)}, u32[]{:S(2)}, u32[]{:S(2)}) collective-permute-start(f32[162,128]{1,0:T(8,128)S(1)} %bitcast.51), channel_id=1, source_target_pairs={{0,4},{4,8},{8,12},{1,5},{5,9},{9,13},{2,6},{6,10},{10,14},{3,7},{... | collective-permute-start | bytes 248840 | tf_op jit(solution)/shard_map/ppermute | solution.py:424
  16.3 1.3 collective-permute-start.1
  17.6 0.0 all-gather.3.cloned.1.call-update
  17.7 0.6 copy.27
  18.3 0.6 dynamic_slice.12.count_ref
  19.0 0.6 constant_dynamic-update-slice_fusion.3
  19.6 3.1 %collective-permute-done.1 = f32[162,128]{1,0:T(8,128)S(1)} collective-permute-done((f32[162,128]{1,0:T(8,128)S(1)}, f32[162,128]{1,0:T(8,128)S(1)}, u32[]{:S(2)}, u32[]{:S(2)}) %collective-permute-start.1) | collective-permute-done | bytes 82976 | tf_op jit(solution)/shard_map/ppermute | solution.py:425
  22.7 0.3 fusion.14
  23.1 0.4 copy-done.4
  23.6 0.3 fusion.15
  23.9 0.7 fusion.5
  24.6 0.3 fusion.16
  24.9 0.3 fusion.17
  25.3 1.7 %fusion.13.block_ref = bf16[128,16,128]{2,1,0:T(8,128)(2,1)} fusion(f32[16,128,1]{2,0,1:T(8,128)S(1)} %get-tuple-element.19, f32[16,128,127]{2,0,1:T(8,128)S(1)} %get-tuple-element.21, f32[16,128,127]{2,0,1:T(8,128)S(1)} %get-tuple-element.20, f32[16,128,1]{2,0,1:T(8,128)S(1)} %get-tuple-element.18, f32[16,130,128]{2,0,1:T(8,128)S(1)} %fusion.5, ...), kind=kLoop, calls=%fused_computation.15 | loop fusion | flops 2883584 | bytes 5898240 | tf_op jit(solution)/shard_map/transpose | solution.py:448
  27.0 18.8 %shard_map.104.field_ref = bf16[4,128,16,128]{3,2,1,0:T(8,128)(2,1)} custom-call(bf16[128,16,128]{2,1,0:T(8,128)(2,1)} %fusion.13.block_ref), custom_call_target="tpu_custom_call" | custom-call | tf_op jit(solution)/shard_map/pallas_call | solution.py:291
  45.8 19.8 %shard_map.105.block_ref.own_ref = bf16[64,8192]{1,0:T(8,128)(2,1)} custom-call(s32[8192]{0:T(1024)} %cell_ref.1, bf16[4,128,16,128]{3,2,1,0:T(8,128)(2,1)} %shard_map.104.field_ref), custom_call_target="tpu_custom_call" | custom-call | flops 100000000 | bytes 4194304 | tf_op jit(solution)/shard_map/pallas_call | solution.py:452
  65.6 18.1 %shard_map.106 = (bf16[64,8192]{1,0:T(8,128)(2,1)}, bf16[64,8192]{1,0:T(8,128)(2,1)}) custom-call(bf16[64,8192]{1,0:T(8,128)(2,1)} %shard_map.105.block_ref.own_ref), custom_call_target="tpu_custom_call" | custom-call | tf_op jit(solution)/shard_map/pallas_call | solution.py:391
  83.7 0.7 pad_maximum_fusion.info_ref
  84.4 45.7 %shard_map.107.block_ref = bf16[32,32,128]{2,1,0:T(8,128)(2,1)} custom-call(s32[32]{0:T(128)} %dynamic_slice.12.count_ref, s32[16384]{0:T(1024)} %bitcast.48, bf16[64,8192]{1,0:T(8,128)(2,1)} %get-tuple-element.6.before_ref, bf16[64,8192]{1,0:T(8,128)(2,1)} %shard_map.105.block_ref.own_ref, bf16[64,8192]{1,0:T(8,128)(2,1)} %get-tuple-element.7.after_ref, ...), custom_call_target="tpu_custom_call" | custom-call | flops 1000000000 | bytes 4194304 | tf_op jit(solution)/shard_map/pallas_call | solution.py:464
  130.1 9.3 %shard_map.108 = bf16[4,32,32,128]{3,2,1,0:T(8,128)(2,1)} custom-call(bf16[32,32,128]{2,1,0:T(8,128)(2,1)} %shard_map.107.block_ref), custom_call_target="tpu_custom_call" | custom-call | tf_op jit(solution)/shard_map/pallas_call | solution.py:291
  139.5 2.2 %constant_dynamic-slice_fusion.field_mix_ref = bf16[128,16,64]{2,1,0:T(8,128)(2,1)} fusion(bf16[128,32,128]{2,1,0:T(8,128)(2,1)} %bitcast.37, s32[]{:T(128)S(6)} %select_n.27, s32[]{:T(128)S(6)} %select_n.29), kind=kLoop, calls=%fused_computation.33 | loop fusion | bytes 524296 | tf_op jit(solution)/shard_map/dynamic_slice | solution.py:484
  141.7 1.3 constant_dynamic-slice_fusion.1.snap_mix_ref
  143.0 4.3 %copy.17 = bf16[256,32,128]{2,1,0:T(8,128)(2,1)} copy(bf16[256,32,128]{2,0,1:T(8,128)(2,1)} %all-gather.3.cloned.1.call-done) | data formatting | bytes 4194304 | tf_op jit(solution)/shard_map/all_gather | solution.py:489
  147.3 8.9 %shard_map.109 = (bf16[128,32,128]{2,1,0:T(8,128)(2,1)}, bf16[128,16,128]{2,1,0:T(8,128)(2,1)}) custom-call(bf16[2,128,32,128]{3,2,1,0:T(8,128)(2,1)} %bitcast.36, bf16[128,32,64]{2,1,0:T(8,128)(2,1)} %constant_dynamic-slice_fusion.1.snap_mix_ref, bf16[4,128,16,128]{3,2,1,0:T(8,128)(2,1)} %shard_map.104.field_ref, ...), custom_call_target="tpu_custom_call" | custom-call | flops 100000000 | bytes 4194304 | tf_op jit(solution)/shard_map/pallas_call | solution.py:490
  156.2 2.7 %copy.25 = bf16[1,32,128,128]{3,2,1,0:T(8,128)(2,1)} copy(bf16[1,32,128,128]{3,1,2,0:T(8,128)(2,1)} %bitcast.40) | data formatting | bytes 2097152
  158.9 0.9 copy.26
  (30 shorter events, 0.1 us)
Async XLA Ops:
  7.2 10.5 %copy-start = (s32[128,512]{1,0:T(8,128)S(1)}, s32[128,512]{1,0:T(8,128)}, u32[]{:S(2)}) copy-start(s32[128,512]{1,0:T(8,128)} %param.16) | copy-start | bytes 786436
  7.2 11.8 %copy-start.2 = (f32[16,128,128]{2,1,0:T(8,128)S(1)}, f32[16,128,128]{2,1,0:T(8,128)}, u32[]{:S(2)}) copy-start(f32[16,128,128]{2,1,0:T(8,128)} %param.10) | copy-start | bytes 3145732
  7.2 11.2 %copy-start.7 = (s32[128]{0:T(128)S(1)}, s32[128]{0:T(128)}, u32[]{:S(2)}) copy-start(s32[128]{0:T(128)} %param.17) | copy-start | bytes 1540
  7.2 135.8 %all-gather.3.cloned.1.call-start = ((), (), s32[]{:S(2)}) async-start(), calls=%async_computation | async-start | bytes 3145728 | tf_op jit(solution)/shard_map/all_gather | solution.py:489
  11.4 7.6 %collective-permute-start = (f32[162,128]{1,0:T(8,128)S(1)}, f32[162,128]{1,0:T(8,128)S(1)}, u32[]{:S(2)}, u32[]{:S(2)}) collective-permute-start(f32[162,128]{1,0:T(8,128)S(1)} %bitcast.51), channel_id=1, source_target_pairs={{0,4},{4,8},{8,12},{1,5},{5,9},{9,13},{2,6},{6,10},{10,14},{3,7},{... | collective-permute-start | bytes 248840 | tf_op jit(solution)/shard_map/ppermute | solution.py:424
  16.3 6.4 %collective-permute-start.1 = (f32[162,128]{1,0:T(8,128)S(1)}, f32[162,128]{1,0:T(8,128)S(1)}, u32[]{:S(2)}, u32[]{:S(2)}) collective-permute-start(f32[162,128]{1,0:T(8,128)S(1)} %bitcast.52), channel_id=1, source_target_pairs={{4,0},{8,4},{12,8},{5,1},{9,5},{13,9},{6,2},{10,6},{14,10},{7,3},{... | collective-permute-start | bytes 248840 | tf_op jit(solution)/shard_map/ppermute | solution.py:425
  22.7 0.8 copy-start.4
  65.6 18.1 %copy-start.5 = (f32[8192]{0:T(1024)S(1)}, f32[8192]{0:T(1024)}, u32[]{:S(2)}) copy-start(f32[8192]{0:T(1024)} %param.14) | copy-start | bytes 98308
  65.6 18.1 %copy-start.6 = (f32[8192]{0:T(1024)S(1)}, f32[8192]{0:T(1024)}, u32[]{:S(2)}) copy-start(f32[8192]{0:T(1024)} %param.15) | copy-start | bytes 98308
  139.4 2.2 %copy-start.1 = (bf16[4,32,32,128]{3,2,1,0:T(8,128)(2,1)S(1)}, bf16[4,32,32,128]{3,2,1,0:T(8,128)(2,1)}, u32[]{:S(2)}) copy-start(bf16[4,32,32,128]{3,2,1,0:T(8,128)(2,1)} %shard_map.108) | copy-start | bytes 3145732
  156.2 2.7 %copy-start.3 = (bf16[128,16,128]{2,1,0:T(8,128)(2,1)S(1)}, bf16[128,16,128]{2,1,0:T(8,128)(2,1)}, u32[]{:S(2)}) copy-start(bf16[128,16,128]{2,1,0:T(8,128)(2,1)} %get-tuple-element.9) | copy-start | bytes 1572868
Sparse Core Ops, SparseCore 0:
  17.8 13.5 all-gather.2

commit v4 on v3

--- a/solution.py
+++ b/solution.py
@@ -80,19 +80,20 @@
 
 
 def mixing_kernel(
-    count_ref, index_ref, before_ref, own_ref, after_ref, info_ref, out_ref,
+    count_ref, index_ref, window_ref, info_ref, out_ref,
     table, picked, gram, chol, inv, wide,
 ):
     share = count_ref.shape[0]
     entries = index_ref.shape[0] // share
-    members, obs = own_ref.shape
+    members, obs = window_ref.shape[2:]
     blocks = obs // LANES
     eye = identity()
 
-    for part, ref in enumerate((before_ref, own_ref, after_ref)):
-
-        def build(b, carry, part=part, ref=ref):
-            sample = ref[:, pl.ds(pl.multiple_of(b * LANES, LANES), LANES)].astype(jnp.float32)
+    for part in range(6):
+
+        def build(b, carry, part=part):
+            start = pl.multiple_of(b * LANES, LANES)
+            sample = window_ref[part // 2, part % 2, :, pl.ds(start, LANES)].astype(jnp.float32)
             mean = jnp.sum(sample, axis=0, keepdims=True) * (1.0 / members)
             value = info_ref[0, pl.ds(part * blocks + b, 1), :]
             weight = info_ref[1, pl.ds(part * blocks + b, 1), :]
@@ -298,11 +299,10 @@
     )(block)
 
 
-def halo_kernel(block_ref, before_ref, after_ref, send_sem, recv_sem, pass_send, pass_recv):
+def halo_kernel(block_ref, window_ref, own_send, own_recv, send_sem, recv_sem, pass_send, pass_recv):
     region, core = lax.axis_index("region"), lax.axis_index("member")
     regions = lax.axis_size("region")
-    half = block_ref.shape[0] // 2
-    size = half // 2
+    size = block_ref.shape[0] // 2
     other = {"member": 1 - core}
     has_before = region > 0
     has_after = region < regions - 1
@@ -325,12 +325,12 @@
     pl.semaphore_wait(barrier, peers)
 
     def rows(c):
-        return pl.ds(pl.multiple_of(core * half + c * size, 16), size)
+        return pl.ds(c * size, size)
 
     def to_side(side, c):
         return pltpu.make_async_remote_copy(
             src_ref=block_ref.at[rows(c)],
-            dst_ref=(before_ref, after_ref)[side].at[rows(c)],
+            dst_ref=window_ref.at[2 * side, core, rows(c)],
             send_sem=send_sem.at[side, c],
             recv_sem=recv_sem.at[side, c],
             device_id={"region": region + 1 - 2 * side},
@@ -338,7 +338,7 @@
         )
 
     def onward(side, c):
-        ref = (before_ref, after_ref)[side]
+        ref = window_ref.at[2 * side, core]
         return pltpu.make_async_remote_copy(
             src_ref=ref.at[rows(c)],
             dst_ref=ref.at[rows(c)],
@@ -357,11 +357,21 @@
             for c in range(2):
                 to_side(side, c).start()
 
-    for side, ref in enumerate((before_ref, after_ref)):
+    beside = pltpu.make_async_remote_copy(
+        src_ref=block_ref,
+        dst_ref=window_ref.at[1, core],
+        send_sem=own_send,
+        recv_sem=own_recv,
+        device_id=other,
+        device_id_type=MESH,
+    )
+    beside.start()
+    window_ref[1, core] = block_ref[...]
+    for side in range(2):
 
         @pl.when(jnp.logical_not(receives[side]))
-        def _(ref=ref):
-            ref[...] = jnp.zeros_like(ref)
+        def _(side=side):
+            window_ref[2 * side] = jnp.zeros(window_ref.shape[1:], window_ref.dtype)
 
     for c in range(2):
         for side in range(2):
@@ -383,17 +393,20 @@
             for c in range(2):
                 onward(side, c).wait()
 
+    beside.wait()
+
 
 def sample_halo(block, collective_id):
     sems = pltpu.SemaphoreType.DMA((2, 2))
     vmem = pl.BlockSpec(memory_space=pltpu.VMEM)
-    shape = jax.ShapeDtypeStruct(block.shape, block.dtype)
+    shape = jax.ShapeDtypeStruct((3, 2) + block.shape, block.dtype)
+    one = pltpu.SemaphoreType.DMA
     return pl.pallas_call(
         halo_kernel,
-        out_shape=(shape, shape),
+        out_shape=shape,
         in_specs=[vmem],
-        out_specs=(vmem, vmem),
-        scratch_shapes=[sems, sems, sems, sems],
+        out_specs=vmem,
+        scratch_shapes=[one, one, sems, sems, sems, sems],
         compiler_params=pltpu.CompilerParams(
             collective_id=collective_id, has_side_effects=True, vmem_limit_bytes=VMEM_BYTES
         ),
@@ -449,14 +462,17 @@
     everyone = group_gather(by_row, 1)
     members = group_size * own_members
     vmem, smem = pltpu.VMEM, pltpu.SMEM
+    my_cell = lax.dynamic_slice_in_dim(
+        obs_cell, lax.axis_index("member") * (obs_count // 2), obs_count // 2, 0
+    )
     sampled = vmem_call(
         sample_kernel,
-        jax.ShapeDtypeStruct((members, obs_count), jnp.bfloat16),
+        jax.ShapeDtypeStruct((members, obs_count // 2), jnp.bfloat16),
         [pltpu.VMEM((rows * cols, LANES), jnp.float32), pltpu.VMEM((LANES, LANES), jnp.float32)],
         (smem, vmem),
         10**8,
-    )(obs_cell, everyone)
-    before, after = sample_halo(sampled, 2)
+    )(my_cell, everyone)
+    window = sample_halo(sampled, 2)
     share = tile_obs.shape[0] // group_size
     first_tile = group_rank * share
     my_index = lax.dynamic_slice_in_dim(tile_obs, first_tile, share, 0).reshape(-1)
@@ -472,9 +488,9 @@
             pltpu.VMEM((members, members, share), jnp.float32),
             pltpu.VMEM((share, members, members), jnp.float32),
         ],
-        (smem, smem, vmem, vmem, vmem, vmem),
+        (smem, smem, vmem, vmem),
         10**9,
-    )(my_count, my_index, before, sampled, after, window_info)
+    )(my_count, my_index, window, window_info)
     mixing = group_gather(mine, 3)
     mixing = mixing.reshape(-1, members // 2, 2 * members)
     member_rank = lax.axis_index("member")

time: 170 us -> 164 us (0.965); the launches traced: 167 us -> 163 us
  Pallas kernels: 121 us -> 117 us
    pallas_call x2, Pallas kernels: 37.9 us -> 32 us  [the longest x1 18.2 us: sample_halo(): pl.pallas_call(halo_kernel, out_shape=shape, in_specs=[vmem], out_specs=v...]
    pallas_call x2, Pallas kernels: 28.1 us -> 33.3 us  [group_gather(): pl.pallas_call(gather_kernel, out_shape=jax.ShapeDtypeStruct((lags * 2,)...]
    pallas_call x1, Pallas kernels: 45.7 us -> 43.1 us  [local(): vmem_call(mixing_kernel, jax.ShapeDtypeStruct((share, members // 2, 2 * m...]
    unnamed x26 -> x28, local copies, waits for them, and re-layouts: 6.86 us -> 6.84 us
  transfers between devices with their start and end apart: 3 -> 3, of which waited for: 1 -> 1; matrix products, arithmetic and copies ran while one was open for 6% -> 6% of each run, Pallas kernels for 67% -> 66%
where the time goes in v4:
time: 164 us; the launch traced here: 163 us
  Pallas kernels  117 us (71%)
  local copies, waits for them, and re-layouts  19 us (12%)
  between operations  14.3 us (9%)
  starting transfers between devices  6.26 us (4%)
  other arithmetic  3.98 us (2%)
  waiting for transfers between devices  2.57 us (2%)
    pallas_call x1, Pallas kernels, local(): vmem_call(mixing_kernel, jax.ShapeDtypeStruct((share, members // 2, 2 * m...  43.1 us
    pallas_call x2, Pallas kernels, group_gather(): pl.pallas_call(gather_kernel, out_shape=jax.ShapeDtypeStruct((lags * 2,)...  33.3 us
    pallas_call x1, Pallas kernels, sample_halo(): pl.pallas_call(halo_kernel, out_shape=shape, in_specs=[vmem], out_specs=v...  18.2 us
    pallas_call x1, Pallas kernels, local(): vmem_call(sample_kernel, jax.ShapeDtypeStruct((members, obs_count // 2),...  13.8 us
    pallas_call x1, Pallas kernels, local(): vmem_call(update_kernel, (jax.ShapeDtypeStruct((rows, half_members, cols)...  8.84 us
    unnamed x28, local copies, waits for them, and re-layouts  6.84 us
    ppermute x1, starting transfers between devices, local(): before = lax.ppermute(edge(rows - depth, rows - depth + 1), 'region', up)  4.93 us
    all_gather x1, local copies, waits for them, and re-layouts, local(): snaps = lax.all_gather(snapshots[0].transpose(1, 0, 2), 'member', axis=0)  4.28 us
  transfers between devices with their start and end apart: 3, of which 1 were waited for; matrix products, arithmetic and copies ran while one was open for 6% of the time, Pallas kernels for 66%

profile of v4, /device:TPU:0, one launch (start us, length us, event | category | flops | bytes accessed | tf_op | source)
XLA Modules:
  0.0 163.3 jit_solution(16684325292506285806)
XLA Ops:
  7.2 0.0 all-gather.3.cloned.1.call-start
  7.3 1.0 fusion.18
  8.2 0.8 convert_element_type.6
  9.1 0.7 constant_dynamic-update-slice_fusion.12
  9.8 0.8 constant_dynamic-update-slice_fusion.8
  10.6 0.8 constant_dynamic-update-slice_fusion.6
  11.4 4.9 %collective-permute-start = (f32[162,128]{1,0:T(8,128)S(1)}, f32[162,128]{1,0:T(8,128)S(1)}, u32[]{:S(2)}, u32[]{:S(2)}) collective-permute-start(f32[162,128]{1,0:T(8,128)S(1)} %bitcast.51), channel_id=1, source_target_pairs={{0,4},{4,8},{8,12},{1,5},{5,9},{9,13},{2,6},{6,10},{10,14},{3,7},{... | collective-permute-start | bytes 248840 | tf_op jit(solution)/shard_map/ppermute | solution.py:437
  16.3 1.3 collective-permute-start.1
  17.7 0.6 copy.27
  18.3 0.6 dynamic_slice.15.count_ref
  18.9 0.6 dynamic_slice.17.cell_ref
  19.5 0.6 constant_dynamic-update-slice_fusion.3
  20.1 2.5 %collective-permute-done.1 = f32[162,128]{1,0:T(8,128)S(1)} collective-permute-done((f32[162,128]{1,0:T(8,128)S(1)}, f32[162,128]{1,0:T(8,128)S(1)}, u32[]{:S(2)}, u32[]{:S(2)}) %collective-permute-start.1) | collective-permute-done | bytes 82976 | tf_op jit(solution)/shard_map/ppermute | solution.py:438
  22.7 0.3 fusion.14
  23.1 0.4 copy-done.4
  23.5 0.3 fusion.15
  23.9 0.7 fusion.5
  24.6 0.3 fusion.16
  24.9 0.3 fusion.17
  25.2 1.7 %fusion.13.block_ref = bf16[128,16,128]{2,1,0:T(8,128)(2,1)} fusion(f32[16,128,1]{2,0,1:T(8,128)S(1)} %get-tuple-element.15, f32[16,128,127]{2,0,1:T(8,128)S(1)} %get-tuple-element.17, f32[16,128,127]{2,0,1:T(8,128)S(1)} %get-tuple-element.16, f32[16,128,1]{2,0,1:T(8,128)S(1)} %get-tuple-element.14, f32[16,130,128]{2,0,1:T(8,128)S(1)} %fusion.5, ...), kind=kLoop, calls=%fused_computation.15 | loop fusion | flops 2883584 | bytes 5898240 | tf_op jit(solution)/shard_map/transpose | solution.py:461
  27.0 18.8 %shard_map.104.field_ref = bf16[4,128,16,128]{3,2,1,0:T(8,128)(2,1)} custom-call(bf16[128,16,128]{2,1,0:T(8,128)(2,1)} %fusion.13.block_ref), custom_call_target="tpu_custom_call" | custom-call | tf_op jit(solution)/shard_map/pallas_call | solution.py:292
  45.8 13.8 %shard_map.105.block_ref = bf16[64,4096]{1,0:T(8,128)(2,1)} custom-call(s32[4096]{0:T(1024)} %dynamic_slice.17.cell_ref, bf16[4,128,16,128]{3,2,1,0:T(8,128)(2,1)} %shard_map.104.field_ref), custom_call_target="tpu_custom_call" | custom-call | flops 100000000 | bytes 4194304 | tf_op jit(solution)/shard_map/pallas_call | solution.py:468
  59.6 18.2 %shard_map.106.window_ref = bf16[3,2,64,4096]{3,2,1,0:T(8,128)(2,1)} custom-call(bf16[64,4096]{1,0:T(8,128)(2,1)} %shard_map.105.block_ref), custom_call_target="tpu_custom_call" | custom-call | tf_op jit(solution)/shard_map/pallas_call | solution.py:404
  77.8 0.7 pad_maximum_fusion.info_ref
  78.5 43.1 %shard_map.107.block_ref = bf16[32,32,128]{2,1,0:T(8,128)(2,1)} custom-call(s32[32]{0:T(128)} %dynamic_slice.15.count_ref, s32[16384]{0:T(1024)} %bitcast.48, bf16[3,2,64,4096]{3,2,1,0:T(8,128)(2,1)} %shard_map.106.window_ref, f32[2,192,128]{2,1,0:T(8,128)} %pad_maximum_fusion.info_ref), custom_call_target="tpu_custom_call" | custom-call | flops 1000000000 | bytes 4194304 | tf_op jit(solution)/shard_map/pallas_call | solution.py:480
  121.6 14.5 %shard_map.108 = bf16[4,32,32,128]{3,2,1,0:T(8,128)(2,1)} custom-call(bf16[32,32,128]{2,1,0:T(8,128)(2,1)} %shard_map.107.block_ref), custom_call_target="tpu_custom_call" | custom-call | tf_op jit(solution)/shard_map/pallas_call | solution.py:292
  136.2 2.2 %constant_dynamic-slice_fusion.field_mix_ref = bf16[128,16,64]{2,1,0:T(8,128)(2,1)} fusion(bf16[128,32,128]{2,1,0:T(8,128)(2,1)} %bitcast.37, s32[]{:T(128)S(6)} %select_n.31, s32[]{:T(128)S(6)} %select_n.33), kind=kLoop, calls=%fused_computation.33 | loop fusion | bytes 524296 | tf_op jit(solution)/shard_map/dynamic_slice | solution.py:500
  138.4 1.3 constant_dynamic-slice_fusion.1.snap_mix_ref
  139.7 4.3 %copy.17 = bf16[256,32,128]{2,1,0:T(8,128)(2,1)} copy(bf16[256,32,128]{2,0,1:T(8,128)(2,1)} %all-gather.3.cloned.1.call-done) | data formatting | bytes 4194304 | tf_op jit(solution)/shard_map/all_gather | solution.py:505
  144.0 8.8 %shard_map.109 = (bf16[128,32,128]{2,1,0:T(8,128)(2,1)}, bf16[128,16,128]{2,1,0:T(8,128)(2,1)}) custom-call(bf16[2,128,32,128]{3,2,1,0:T(8,128)(2,1)} %bitcast.36, bf16[128,32,64]{2,1,0:T(8,128)(2,1)} %constant_dynamic-slice_fusion.1.snap_mix_ref, bf16[4,128,16,128]{3,2,1,0:T(8,128)(2,1)} %shard_map.104.field_ref, ...), custom_call_target="tpu_custom_call" | custom-call | flops 100000000 | bytes 4194304 | tf_op jit(solution)/shard_map/pallas_call | solution.py:506
  152.9 2.7 %copy.25 = bf16[1,32,128,128]{3,2,1,0:T(8,128)(2,1)} copy(bf16[1,32,128,128]{3,1,2,0:T(8,128)(2,1)} %bitcast.40) | data formatting | bytes 2097152
  155.5 0.9 copy.26
  (33 shorter events, 0.2 us)
Async XLA Ops:
  7.2 10.5 %copy-start = (s32[128,512]{1,0:T(8,128)S(1)}, s32[128,512]{1,0:T(8,128)}, u32[]{:S(2)}) copy-start(s32[128,512]{1,0:T(8,128)} %param.16) | copy-start | bytes 786436
  7.2 12.3 %copy-start.2 = (f32[16,128,128]{2,1,0:T(8,128)S(1)}, f32[16,128,128]{2,1,0:T(8,128)}, u32[]{:S(2)}) copy-start(f32[16,128,128]{2,1,0:T(8,128)} %param.10) | copy-start | bytes 3145732
  7.2 11.1 %copy-start.8 = (s32[128]{0:T(128)S(1)}, s32[128]{0:T(128)}, u32[]{:S(2)}) copy-start(s32[128]{0:T(128)} %param.17) | copy-start | bytes 1540
  7.2 11.7 %copy-start.7 = (s32[8192]{0:T(1024)S(1)}, s32[8192]{0:T(1024)}, u32[]{:S(2)}) copy-start(s32[8192]{0:T(1024)} %param.13) | copy-start | bytes 98308
  7.2 132.5 %all-gather.3.cloned.1.call-start = ((), (), s32[]{:S(2)}) async-start(), calls=%async_computation | async-start | bytes 3145728 | tf_op jit(solution)/shard_map/all_gather | solution.py:505
  11.4 8.1 %collective-permute-start = (f32[162,128]{1,0:T(8,128)S(1)}, f32[162,128]{1,0:T(8,128)S(1)}, u32[]{:S(2)}, u32[]{:S(2)}) collective-permute-start(f32[162,128]{1,0:T(8,128)S(1)} %bitcast.51), channel_id=1, source_target_pairs={{0,4},{4,8},{8,12},{1,5},{5,9},{9,13},{2,6},{6,10},{10,14},{3,7},{... | collective-permute-start | bytes 248840 | tf_op jit(solution)/shard_map/ppermute | solution.py:437
  16.3 6.4 %collective-permute-start.1 = (f32[162,128]{1,0:T(8,128)S(1)}, f32[162,128]{1,0:T(8,128)S(1)}, u32[]{:S(2)}, u32[]{:S(2)}) collective-permute-start(f32[162,128]{1,0:T(8,128)S(1)} %bitcast.52), channel_id=1, source_target_pairs={{4,0},{8,4},{12,8},{5,1},{9,5},{13,9},{6,2},{10,6},{14,10},{7,3},{... | collective-permute-start | bytes 248840 | tf_op jit(solution)/shard_map/ppermute | solution.py:438
  22.7 0.8 copy-start.4
  59.6 18.2 %copy-start.5 = (f32[8192]{0:T(1024)S(1)}, f32[8192]{0:T(1024)}, u32[]{:S(2)}) copy-start(f32[8192]{0:T(1024)} %param.14) | copy-start | bytes 98308
  59.6 18.2 %copy-start.6 = (f32[8192]{0:T(1024)S(1)}, f32[8192]{0:T(1024)}, u32[]{:S(2)}) copy-start(f32[8192]{0:T(1024)} %param.15) | copy-start | bytes 98308
  136.2 2.2 %copy-start.1 = (bf16[4,32,32,128]{3,2,1,0:T(8,128)(2,1)S(1)}, bf16[4,32,32,128]{3,2,1,0:T(8,128)(2,1)}, u32[]{:S(2)}) copy-start(bf16[4,32,32,128]{3,2,1,0:T(8,128)(2,1)} %shard_map.108) | copy-start | bytes 3145732
  152.8 2.7 %copy-start.3 = (bf16[128,16,128]{2,1,0:T(8,128)(2,1)S(1)}, bf16[128,16,128]{2,1,0:T(8,128)(2,1)}, u32[]{:S(2)}) copy-start(bf16[128,16,128]{2,1,0:T(8,128)(2,1)} %get-tuple-element.5) | copy-start | bytes 1572868
Sparse Core Ops, SparseCore 0:
  17.7 13.5 all-gather.2
